TPU v7x, 128 devices: a whole 4x4x4 slice. The times are simulated.
128 devices in a mesh: dp: 32 (over z, y, core), ctx: 4 (over x).
Axes of the slice: x: 4, y: 4, z: 4, core: 2. Of those that a mesh axis runs over, the one named last changes fastest.
Arguments:
- tokens: bfloat16 [32, 1024, 1088], P('dp', 'ctx'), may hold values from -6 to 6
- cotangent: bfloat16 [32, 1024, 1088], P('dp', 'ctx'), may hold values from -12 to 12
- positions: int32 [32, 1024], P('dp', 'ctx'), may hold values from 0 to 1023, as said below
- w_qkv: float32 [1088, 3264], P('dp', 'ctx'), may hold values from -0.12126781 to 0.12126781
- w_out: float32 [1088, 1088], P('dp', 'ctx'), may hold values from -1.5 to 1.5
- w_up: float32 [1088, 4352], P('dp', 'ctx'), may hold values from -0.210096485 to 0.210096485
- w_down: float32 [4352, 1088], P('dp', 'ctx'), may hold values from -0.052599914 to 0.052599914
- vectors: float32 [1088, 12], P('dp', 'ctx'), may hold values from -1.2 to 4.2
- moment_qkv: float32 [1088, 3264], P('dp', 'ctx'), may hold values from -0.00018310547 to 0.00018310547
- square_qkv: float32 [1088, 3264], P('dp', 'ctx'), may hold values from 1.1235538e-11 to 4.5026628e-11
- moment_out: float32 [1088, 1088], P('dp', 'ctx'), may hold values from -6.1035156e-05 to 6.1035156e-05
- square_out: float32 [1088, 1088], P('dp', 'ctx'), may hold values from 1.5881812e-12 to 6.3358294e-12
- moment_up: float32 [1088, 4352], P('dp', 'ctx'), may hold values from -0.00030517578 to 0.00030517578
- square_up: float32 [1088, 4352], P('dp', 'ctx'), may hold values from 3.4466912e-11 to 1.3769869e-10
- moment_down: float32 [4352, 1088], P('dp', 'ctx'), may hold values from -0.00061035156 to 0.00061035156
- square_down: float32 [4352, 1088], P('dp', 'ctx'), may hold values from 1.5881813e-10 to 6.3358296e-10
- moment_vec: float32 [1088, 12], P('dp', 'ctx'), may hold values from -0.00036621094 to 0.00036621094
- square_vec: float32 [1088, 12], P('dp', 'ctx'), may hold values from 4.5026628e-11 to 1.7993755e-10
Outputs:
- outputs: bfloat16 [32, 1024, 1088], P('dp', 'ctx')
- d_tokens: float32 [32, 1024, 1088], P('dp', 'ctx')
- grad_norm: float32 [], replicated
- first_qkv: float32 [1088, 3264], P('dp', 'ctx')
- second_qkv: float32 [1088, 3264], P('dp', 'ctx')
- updated_qkv: float32 [1088, 3264], P('dp', 'ctx')
- first_out: float32 [1088, 1088], P('dp', 'ctx')
- second_out: float32 [1088, 1088], P('dp', 'ctx')
- updated_out: float32 [1088, 1088], P('dp', 'ctx')
- first_up: float32 [1088, 4352], P('dp', 'ctx')
- second_up: float32 [1088, 4352], P('dp', 'ctx')
- updated_up: float32 [1088, 4352], P('dp', 'ctx')
- first_down: float32 [4352, 1088], P('dp', 'ctx')
- second_down: float32 [4352, 1088], P('dp', 'ctx')
- updated_down: float32 [4352, 1088], P('dp', 'ctx')
- first_vec: float32 [1088, 12], P('dp', 'ctx')
- second_vec: float32 [1088, 12], P('dp', 'ctx')
- updated_vec: float32 [1088, 12], P('dp', 'ctx')
Inputs may be any that keep to these rules, and one draw needn't show every extreme that they name: positions is 0 at the first token of every sequence and of every document and rises by one within a document; documents hold 200 to 2000 tokens, except the first and last of a sequence, which may be cut short.
All inputs are finite; a program needn't handle non-finite values.
Results may differ from a plain program's by a relative error of at most 0.013.
The roundings to bfloat16 on the way count: a program that leaves them out, or rounds other values in their place, can miss the bound.
Values may be sent and summed in bfloat16 or wider, within the bound.
No kernel may reach another device: no remote copies, remote signals or barrier semaphores. Data moves between devices by JAX's collectives and lax.ppermute only.
A program may use at most 192 MiB of HBM per device.

v0:
```python
import jax
import jax.numpy as jnp
from jax import lax
from jax.sharding import PartitionSpec as P

HEADS = 17
HEAD_DIM = 64
FF = 4352
STEP = 10


NORM_EPS = 1e-05
ADAM_EPS = 1e-08
BETA_FIRST = 0.9
BETA_SECOND = 0.999
CLIP_LIMIT = 1.0
GELU_SCALE = 0.7978845608
GELU_CUBIC = 0.044715
MASK_FILL = -1e30
LEARN_RATES = (0.05, 0.5, 0.1, 0.03, 1.0)
WEIGHT_DECAYS = (0.1, 0.1, 0.1, 0.1, 0.0)


def layer_norm(inputs, gain_col, shift_col):
    centre = inputs - jnp.mean(inputs, axis=-1, keepdims=True)
    spread = jnp.mean(centre * centre, axis=-1, keepdims=True)
    return centre * lax.rsqrt(spread + NORM_EPS) * gain_col + shift_col


def gelu(inputs):
    inner = GELU_SCALE * (inputs + GELU_CUBIC * inputs * inputs * inputs)
    return 0.5 * inputs * (1.0 + jnp.tanh(inner))


def adam_step(weight, moment, square, gradient, rate, decay):
    first = BETA_FIRST * moment + (1.0 - BETA_FIRST) * gradient
    second = BETA_SECOND * square + (1.0 - BETA_SECOND) * gradient * gradient
    first_hat = first / (1.0 - BETA_FIRST**STEP)
    second_hat = second / (1.0 - BETA_SECOND**STEP)
    updated = weight - rate * (first_hat / (jnp.sqrt(second_hat) + ADAM_EPS) + decay * weight)
    return (first, second, updated)


def contract_last(left_side, right_side):
    return lax.dot_general(
        left_side, right_side, (((1,), (1,)), ((), ())), preferred_element_type=jnp.float32
    )


def contract_first(left_side, right_side):
    return lax.dot_general(
        left_side, right_side, (((0,), (0,)), ((), ())), preferred_element_type=jnp.float32
    )


def masked_scores(query_h, key_h, query_pos, first_index):
    scores = contract_last(query_h, key_h) * HEAD_DIM ** (-0.5)
    query_index = first_index + jnp.arange(query_h.shape[0], dtype=jnp.int32)
    key_index = jnp.arange(key_h.shape[0], dtype=jnp.int32)
    allowed = (key_index[None, :] <= query_index[:, None]) & (
        key_index[None, :] >= (query_index - query_pos)[:, None]
    )
    return jnp.where(allowed, scores, MASK_FILL)


def body(
    tokens,
    cotangent,
    positions,
    w_qkv,
    w_out,
    w_up,
    w_down,
    vectors,
    moment_qkv,
    square_qkv,
    moment_out,
    square_out,
    moment_up,
    square_up,
    moment_down,
    square_down,
    moment_vec,
    square_vec,
):
    seq_count, local_len, model_width = tokens.shape
    row_count = seq_count * local_len
    ctx_count = lax.axis_size("ctx")
    dp_count = lax.axis_size("dp")
    ctx_rank = lax.axis_index("ctx")
    dp_rank = lax.axis_index("dp")
    full_len = local_len * ctx_count
    first_index = ctx_rank * local_len
    inputs = tokens.reshape(row_count, model_width).astype(jnp.float32)
    shards_low = (
        w_qkv.astype(jnp.bfloat16),
        w_out.astype(jnp.bfloat16),
        w_up.astype(jnp.bfloat16),
        w_down.astype(jnp.bfloat16),
        vectors.astype(jnp.bfloat16),
    )
    qkv_cols, out_cols, up_cols, down_cols, vec_cols = (
        lax.all_gather(shards_low[0], "ctx", axis=1, tiled=True),
        lax.all_gather(shards_low[1], "ctx", axis=1, tiled=True),
        lax.all_gather(shards_low[2], "ctx", axis=1, tiled=True),
        lax.all_gather(shards_low[3], "ctx", axis=1, tiled=True),
        lax.all_gather(shards_low[4], "ctx", axis=1, tiled=True),
    )
    centre = inputs - jnp.mean(inputs, axis=-1, keepdims=True)
    normed_one = centre * lax.rsqrt(jnp.mean(centre * centre, axis=-1, keepdims=True) + NORM_EPS)
    weight_piece = lax.all_gather(qkv_cols, "dp", axis=0, tiled=True)
    vec_piece = lax.all_gather(vec_cols, "dp", axis=0, tiled=True)
    gains_in = vec_piece.astype(jnp.float32)
    left_piece = (normed_one * gains_in[:, 0] + gains_in[:, 1]).astype(jnp.bfloat16)
    summed = jnp.dot(left_piece, weight_piece, preferred_element_type=jnp.float32)
    vec_full = vec_piece.astype(jnp.float32)
    a_one = (normed_one * vec_full[:, 0] + vec_full[:, 1]).astype(jnp.bfloat16)
    col_shards = (qkv_cols, out_cols, up_cols, down_cols)

    def project(left_side, slot_index):
        return jnp.dot(
            left_side,
            lax.all_gather(col_shards[slot_index], "dp", axis=0, tiled=True),
            preferred_element_type=jnp.float32,
        )

    def project_back(right_side, slot_index):
        return contract_last(
            right_side, lax.all_gather(col_shards[slot_index], "dp", axis=0, tiled=True)
        )

    def reduce_grad(left_side, right_side):
        row_sums = lax.psum_scatter(
            contract_first(left_side, right_side), "dp", scatter_dimension=0, tiled=True
        )
        return lax.psum_scatter(row_sums, "ctx", scatter_dimension=1, tiled=True)

    queries = (summed[:, :model_width] + vec_full[:, 2]).astype(jnp.bfloat16)
    keys_low = summed[:, model_width : 2 * model_width].astype(jnp.bfloat16)
    values_low = (summed[:, 2 * model_width :] + vec_full[:, 3]).astype(jnp.bfloat16)
    keys_seq, values_seq = (
        lax.all_gather(
            keys_low.reshape(seq_count, local_len, model_width), "ctx", axis=1, tiled=True
        ),
        lax.all_gather(
            values_low.reshape(seq_count, local_len, model_width), "ctx", axis=1, tiled=True
        ),
    )

    def to_heads(arranged, length):
        return (
            arranged.reshape(seq_count, length, HEADS, HEAD_DIM)
            .transpose(0, 2, 1, 3)
            .reshape(seq_count * HEADS, length, HEAD_DIM)
        )

    def from_heads(arranged, length):
        return (
            arranged.reshape(seq_count, HEADS, length, HEAD_DIM)
            .transpose(0, 2, 1, 3)
            .reshape(seq_count, length, model_width)
        )

    query_heads = to_heads(queries, local_len)
    key_heads = to_heads(keys_seq, full_len)
    value_heads = to_heads(values_seq, full_len)
    pos_heads = jnp.broadcast_to(positions[:, None, :], (seq_count, HEADS, local_len)).reshape(
        seq_count * HEADS, local_len
    )

    def attend_forward(head_items):
        query_h, key_h, value_h, query_pos = head_items
        scores = masked_scores(query_h, key_h, query_pos, first_index)
        row_peak = jnp.max(scores, axis=-1, keepdims=True)
        exp_terms = jnp.exp(scores - row_peak)
        row_total = jnp.sum(exp_terms, axis=-1, keepdims=True)
        probabilities = exp_terms / row_total
        head_result = jnp.dot(
            probabilities.astype(jnp.bfloat16), value_h, preferred_element_type=jnp.float32
        )
        return (head_result, row_peak, row_total)

    head_out, row_peaks, row_totals = lax.map(
        attend_forward, (query_heads, key_heads, value_heads, pos_heads)
    )
    heads_low = from_heads(head_out, local_len).reshape(row_count, model_width).astype(jnp.bfloat16)
    mixed = inputs + (project(heads_low, 1) + vec_full[:, 4])
    normed_two = layer_norm(mixed, vec_full[:, 5], vec_full[:, 6])
    a_two = normed_two.astype(jnp.bfloat16)
    up_bias = vec_full[:, 7 : 7 + FF // model_width].T.reshape(-1)
    pre_act = project(a_two, 2) + up_bias
    act_low = gelu(pre_act).astype(jnp.bfloat16)
    result = mixed + (project(act_low, 3) + vec_full[:, 11])
    outputs = result.astype(jnp.bfloat16).reshape(seq_count, local_len, model_width)
    cot_low = cotangent.reshape(row_count, model_width)
    cot_full = cot_low.astype(jnp.float32)
    grad_down = reduce_grad(act_low, cot_low)
    d_act = project_back(cot_low, 3)
    unused, gelu_pull = jax.vjp(gelu, pre_act)
    d_pre = gelu_pull(d_act)[0].astype(jnp.bfloat16)
    grad_up = reduce_grad(a_two, d_pre)
    d_two = project_back(d_pre, 2)
    unused, second_pull = jax.vjp(layer_norm, mixed, vec_full[:, 5], vec_full[:, 6])
    d_mixed_part, d_gain_two, d_shift_two = second_pull(d_two)
    d_mixed = cot_full + d_mixed_part
    d_branch = d_mixed.astype(jnp.bfloat16)
    grad_out = reduce_grad(heads_low, d_branch)
    d_heads = project_back(d_branch, 1).astype(jnp.bfloat16)
    grad_heads = to_heads(d_heads, local_len)

    def attend_backward(head_items):
        query_h, key_h, value_h, query_pos, row_peak, row_total, grad_h = head_items
        scores = masked_scores(query_h, key_h, query_pos, first_index)
        probabilities = jnp.exp(scores - row_peak) / row_total
        d_probs = contract_last(grad_h, value_h)
        inner_sum = jnp.sum(d_probs * probabilities, axis=-1, keepdims=True)
        d_scores = (probabilities * (d_probs - inner_sum)).astype(jnp.bfloat16)
        head_scale = HEAD_DIM ** (-0.5)
        d_query = jnp.dot(d_scores, key_h, preferred_element_type=jnp.float32) * head_scale
        d_key = contract_first(d_scores, query_h) * head_scale
        d_value = contract_first(probabilities.astype(jnp.bfloat16), grad_h)
        return (d_query, d_key, d_value)

    d_query_h, d_key_h, d_value_h = lax.map(
        attend_backward,
        (query_heads, key_heads, value_heads, pos_heads, row_peaks, row_totals, grad_heads),
    )
    d_queries = (
        from_heads(d_query_h, local_len).reshape(row_count, model_width).astype(jnp.bfloat16)
    )
    key_sums, value_sums = (
        lax.psum_scatter(from_heads(d_key_h, full_len), "ctx", scatter_dimension=1, tiled=True),
        lax.psum_scatter(from_heads(d_value_h, full_len), "ctx", scatter_dimension=1, tiled=True),
    )
    d_keys = key_sums.reshape(row_count, model_width).astype(jnp.bfloat16)
    d_values = value_sums.reshape(row_count, model_width).astype(jnp.bfloat16)
    d_qkv = jnp.concatenate([d_queries, d_keys, d_values], axis=1)
    grad_qkv = reduce_grad(a_one, d_qkv)
    d_one = project_back(d_qkv, 0)
    unused, first_pull = jax.vjp(layer_norm, inputs, vec_full[:, 0], vec_full[:, 1])
    d_input_part, d_gain_one, d_shift_one = first_pull(d_one)
    d_tokens = (d_mixed + d_input_part).reshape(seq_count, local_len, model_width)
    d_up_bias = jnp.sum(d_pre.astype(jnp.float32), axis=0).reshape(FF // model_width, model_width).T
    vector_terms = jnp.concatenate(
        [
            jnp.stack(
                [
                    d_gain_one,
                    d_shift_one,
                    jnp.sum(d_queries.astype(jnp.float32), axis=0),
                    jnp.sum(d_values.astype(jnp.float32), axis=0),
                    jnp.sum(d_branch.astype(jnp.float32), axis=0),
                    d_gain_two,
                    d_shift_two,
                ],
                axis=1,
            ),
            d_up_bias,
            jnp.sum(cot_full, axis=0)[:, None],
        ],
        axis=1,
    )
    vector_total = lax.psum(vector_terms, ("dp", "ctx"))
    row_size = model_width // dp_count
    col_size = vector_total.shape[1] // ctx_count
    grad_vec = lax.dynamic_slice(
        vector_total, (dp_rank * row_size, ctx_rank * col_size), (row_size, col_size)
    )
    local_sq = (
        jnp.sum(grad_qkv * grad_qkv)
        + jnp.sum(grad_out * grad_out)
        + jnp.sum(grad_up * grad_up)
        + jnp.sum(grad_down * grad_down)
    )
    total_sq = lax.psum(local_sq, ("dp", "ctx")) + jnp.sum(vector_total * vector_total)
    grad_norm = jnp.sqrt(total_sq)
    clip_factor = CLIP_LIMIT / jnp.maximum(grad_norm, CLIP_LIMIT)
    first_qkv, second_qkv, updated_qkv = adam_step(
        w_qkv, moment_qkv, square_qkv, grad_qkv * clip_factor, LEARN_RATES[0], WEIGHT_DECAYS[0]
    )
    first_out, second_out, updated_out = adam_step(
        w_out, moment_out, square_out, grad_out * clip_factor, LEARN_RATES[1], WEIGHT_DECAYS[1]
    )
    first_up, second_up, updated_up = adam_step(
        w_up, moment_up, square_up, grad_up * clip_factor, LEARN_RATES[2], WEIGHT_DECAYS[2]
    )
    first_down, second_down, updated_down = adam_step(
        w_down, moment_down, square_down, grad_down * clip_factor, LEARN_RATES[3], WEIGHT_DECAYS[3]
    )
    first_vec, second_vec, updated_vec = adam_step(
        vectors, moment_vec, square_vec, grad_vec * clip_factor, LEARN_RATES[4], WEIGHT_DECAYS[4]
    )
    return (
        outputs,
        d_tokens,
        grad_norm,
        first_qkv,
        second_qkv,
        updated_qkv,
        first_out,
        second_out,
        updated_out,
        first_up,
        second_up,
        updated_up,
        first_down,
        second_down,
        updated_down,
        first_vec,
        second_vec,
        updated_vec,
    )


def solution(mesh):
    placed = (
        P("dp", "ctx", None),
        P("dp", "ctx", None),
        P("dp", "ctx"),
        P("dp", "ctx"),
        P("dp", "ctx"),
        P("dp", "ctx"),
        P("dp", "ctx"),
        P("dp", "ctx"),
        P("dp", "ctx"),
        P("dp", "ctx"),
        P("dp", "ctx"),
        P("dp", "ctx"),
        P("dp", "ctx"),
        P("dp", "ctx"),
        P("dp", "ctx"),
        P("dp", "ctx"),
        P("dp", "ctx"),
        P("dp", "ctx"),
    )
    return jax.shard_map(
        body,
        mesh=mesh,
        in_specs=placed,
        out_specs=(
            P("dp", "ctx", None),
            P("dp", "ctx", None),
            P(),
            P("dp", "ctx"),
            P("dp", "ctx"),
            P("dp", "ctx"),
            P("dp", "ctx"),
            P("dp", "ctx"),
            P("dp", "ctx"),
            P("dp", "ctx"),
            P("dp", "ctx"),
            P("dp", "ctx"),
            P("dp", "ctx"),
            P("dp", "ctx"),
            P("dp", "ctx"),
            P("dp", "ctx"),
            P("dp", "ctx"),
            P("dp", "ctx"),
        ),
        check_vma=False,
    )
```

profile of v0, /device:TPU:0, one launch (start us, length us, event | category | flops | bytes accessed | tf_op | source)
XLA Modules:
  0.0 1239.8 jit_solution(15249929056463789770)
XLA Ops:
  8.2 12.8 %all-gather.4 = bf16[4,816,34]{1,2,0:T(8,128)(2,1)S(1)} all-gather(bf16[1,816,34]{1,2,0:T(8,128)(2,1)S(1)} %convert_bitcast_fusion.5), channel_id=1, replica_groups=mesh['dp'=32,'ctx'=4] {'ctx'}, dimensions={0}, use_global_device_ids=true | all-gather | bytes 277440 | tf_op jit(solution)/shard_map/all_gather | solution.py:103
  23.0 12.0 all-gather.6
  35.9 9.4 all-gather.2
  45.4 26.1 %all-gather.3 = bf16[32,34,12]{1,2,0:T(8,128)(2,1)S(1)} all-gather(bf16[1,34,12]{1,2,0:T(8,128)(2,1)S(1)} %bitcast.307), channel_id=1, replica_groups=mesh['dp'=32,'ctx'=4] {'dp'}, dimensions={0}, use_global_device_ids=true | all-gather | bytes 26928 | tf_op jit(solution)/shard_map/all_gather | solution.py:112
  78.0 10.0 reshape.244
  88.0 6.8 fusion.96
  100.2 12.7 %all-gather.8 = bf16[4,1088,34]{1,2,0:T(8,128)(2,1)S(1)} all-gather(bf16[1,1088,34]{1,2,0:T(8,128)(2,1)S(1)} %convert_bitcast_fusion.4), channel_id=1, replica_groups=mesh['dp'=32,'ctx'=4] {'ctx'}, dimensions={0}, use_global_device_ids=true | all-gather | bytes 369920 | tf_op jit(solution)/shard_map/all_gather | solution.py:105
  114.3 12.9 %all-gather.10 = bf16[4,272,136]{1,2,0:T(8,128)(2,1)S(1)} all-gather(bf16[1,272,136]{1,2,0:T(8,128)(2,1)S(1)} %convert_bitcast_fusion.3), channel_id=1, replica_groups=mesh['dp'=32,'ctx'=4] {'ctx'}, dimensions={0}, use_global_device_ids=true | all-gather | bytes 369920 | tf_op jit(solution)/shard_map/all_gather | solution.py:106
  134.4 28.2 %all-gather.20.cloned.1.call-done = bf16[1024,1088]{0,1:T(8,128)(2,1)} async-done(((bf16[256,1088]{0,1:T(8,128)(2,1)}), bf16[1024,1088]{0,1:T(8,128)(2,1)}) %all-gather.20.cloned.1.call-update) | async-done | bytes 2228240 | tf_op jit(solution)/shard_map/all_gather | solution.py:142
  167.8 33.4 %all-gather.22.cloned.1.call-done = bf16[1024,1088]{0,1:T(8,128)(2,1)} async-done(((bf16[256,1088]{0,1:T(8,128)(2,1)}), bf16[1024,1088]{0,1:T(8,128)(2,1)}) %all-gather.22.cloned.1.call-update) | async-done | bytes 2228240 | tf_op jit(solution)/shard_map/all_gather | solution.py:145
  206.6 63.9 %while.28 = (s32[]{:T(128)}, bf16[17,256,64]{1,2,0:T(8,128)(2,1)S(1)}, f32[17,256,1]{1,2,0:T(1,128)}, f32[17,256,1]{1,2,0:T(1,128)}, s32[]{:T(128)}, /*index=5*/...) while((s32[]{:T(128)}, ...), condition=%wide.region_5.6_spmd, body=%wide.region_2.5_spmd.sunk | while | flops 69992704 | bytes 3819645 | solution.py:183
  274.2 11.0 reshape.252
  285.2 9.2 convolution_add_fusion
  294.3 28.2 %all-gather.18.cloned.1.call-done = bf16[4352,1088]{1,0:T(8,128)(2,1)} async-done(((bf16[136,1088]{1,0:T(8,128)(2,1)}), bf16[4352,1088]{1,0:T(8,128)(2,1)}) %all-gather.18.cloned.1.call-update) | async-done | bytes 9469968 | tf_op jit(solution)/shard_map/all_gather | solution.py:123
  322.5 8.6 convert_reduce_fusion
  339.0 147.1 %while.29 = (s32[]{:T(128)}, bf16[17,256,64]{1,2,0:T(8,128)(2,1)S(1)}, f32[17,1024,64]{1,2,0:T(8,128)}, f32[17,1024,64]{1,2,0:T(8,128)}, s32[]{:T(128)}, /*index...) while((s32[]{:T(128)}, ...), condition=%wide.region_12.13_spmd, body=%wide.region_10.12_spmd.sunk | while | flops 171262208 | bytes 9523345 | solution.py:224
  486.9 13.8 %fusion.79 = f32[4352,1088]{1,0:T(8,128)} fusion(bf16[1,256,1088]{1,2,0:T(8,128)(2,1)} %param.23, f32[256,4352]{1,0:T(8,128)} %convolution_add_fusion), kind=kOutput, calls=%fused_computation.125 | convolution fusion | flops 2434334720 | bytes 23953408 | tf_op jit(solution)/shard_map/dot_general | solution.py:51
  505.3 8.5 fusion.98
  513.8 20.8 %reduce-scatter.26.cloned.1.call-done = f32[1,256,1088]{1,2,0:T(8,128)} async-done(((f32[1,1024,1088]{1,2,0:T(8,128)}), f32[1,256,1088]{1,2,0:T(8,128)}) %reduce-scatter.26.cloned.1.call-update) | async-done | bytes 1114128 | tf_op jit(solution)/shard_map/reduce_scatter | solution.py:233
  536.8 49.0 %reduce-scatter.24.cloned.1.call-done = f32[1,256,1088]{1,2,0:T(8,128)} async-done(((f32[1,1024,1088]{1,2,0:T(8,128)}), f32[1,256,1088]{1,2,0:T(8,128)}) %reduce-scatter.24.cloned.1.call-update) | async-done | bytes 1114128 | tf_op jit(solution)/shard_map/reduce_scatter | solution.py:232
  587.9 8.5 fusion.77
  596.4 302.5 %fusion.102 = (f32[40,3264]{1,0:T(8,128)}, f32[48,1088]{1,0:T(8,128)}, f32[40,4352]{1,0:T(8,128)S(1)}) fusion(f32[1088,3264]{1,0:T(8,128)} %fusion.77, f32[1088,1088]{1,0:T(8,128)} %fusion.112, f32[1088,4352]{1,0:T(8,128)} %fusion.98), kind=kCustom, calls=%all-reduce-scatter.3 | all-reduce-scatter fusion | flops 11419650 | bytes 39307776
  905.9 7.1 collective-permute-start.11
  950.2 8.6 collective-permute-start.4
  962.2 17.6 %concatenate.9 = f32[482,1088]{1,0:T(8,128)} concatenate(f32[2,1088]{1,0:T(2,128)S(1)} %collective-permute-done.14, f32[48,1088]{1,0:T(8,128)} %collective-permute-done.13, f32[48,1088]{1,0:T(8,128)} %collective-permute-done.12, f32[48,1088]{1,0:T(8,128)} %collective-permute-done.11, f32[48,1088]{1,0:T(8,128)} %collective-permute-done.10, f32[48,1088]{1,0:T(8,128)} %collective-permute-done.9, ...), dimensions={0} | concatenate | bytes 4195328
  1002.1 14.8 %collective-permute-start.19 = (f32[26,4352]{1,0:T(8,128)}, f32[26,4352]{1,0:T(8,128)}, u32[]{:S(2)}, u32[]{:S(2)}) collective-permute-start(f32[26,4352]{1,0:T(8,128)} %slice.67), channel_id=1, source_target_pairs={{0,20},{4,24},{8,28},{12,32},{16,36},{20,40},{24,44},{28,48},{32,5... | collective-permute-start | bytes 1357832
  1016.9 18.2 %concatenate.8 = f32[226,3264]{1,0:T(8,128)} concatenate(f32[26,3264]{1,0:T(8,128)} %collective-permute-done.4, f32[40,3264]{1,0:T(8,128)} %collective-permute-done.3, f32[40,3264]{1,0:T(8,128)} %collective-permute-done.2, f32[40,3264]{1,0:T(8,128)} %collective-permute-done.1, f32[40,3264]{1,0:T(8,128)} %collective-permute-done, f32[40,3264]{1,0:T(8,128)} %get-tuple-element.199), dimensions={0} | concatenate | bytes 5901312
  1045.9 24.4 %concatenate.10 = f32[226,4352]{1,0:T(8,128)} concatenate(f32[26,4352]{1,0:T(8,128)} %collective-permute-done.19, f32[40,4352]{1,0:T(8,128)} %collective-permute-done.18, f32[40,4352]{1,0:T(8,128)} %collective-permute-done.17, f32[40,4352]{1,0:T(8,128)} %collective-permute-done.16, f32[40,4352]{1,0:T(8,128)} %collective-permute-done.15, f32[40,4352]{1,0:T(8,128)S(1)} %get-tuple-element.201), dimensions={0} | concatenate | bytes 7868416
  1093.8 27.1 %reduce-scatter.32.cloned.1.call-done = f32[1088,34]{1,0:T(8,128)} async-done(((f32[4352,34]{1,0:T(8,128)}), f32[1088,34]{1,0:T(8,128)}) %reduce-scatter.32.cloned.1.call-update) | async-done | bytes 147984
  1123.5 23.3 %reduce-scatter.34.cloned.1.call-done = f32[272,136]{1,0:T(8,128)} async-done(((f32[1088,136]{1,0:T(8,128)}), f32[272,136]{1,0:T(8,128)}) %reduce-scatter.34.cloned.1.call-update) | async-done | bytes 147984
  1149.4 10.4 fusion.61
  1159.8 65.8 %all-reduce.7 = (f32[]{:T(128)}, f32[1088,12]{0,1:T(8,128)S(1)}) all-reduce(f32[]{:T(128)S(6)} %add.297, f32[1088,12]{0,1:T(8,128)S(1)} %concatenate.7), channel_id=1, replica_groups=mesh['dp'=32,'ctx'=4] {'dp','ctx'}, use_global_device_ids=true, to_apply=%region_29.30 | all-reduce | flops 13057 | bytes 104456 | tf_op jit(solution)/shard_map/psum | solution.py:275
  (506 shorter events, 376.1 us)
Async XLA Ops:
  7.2 70.8 %all-gather.24.cloned.1.call-start = ((), (), s32[]{:S(2)}) async-start(), calls=%async_computation.12 | async-start | bytes 8785920 | tf_op jit(solution)/shard_map/all_gather | solution.py:111
  22.1 106.9 %all-gather.26.cloned.1.call-start = ((), (), s32[]{:S(2)}) async-start(), calls=%async_computation.13 | async-start | bytes 3041280 | tf_op jit(solution)/shard_map/all_gather | solution.py:123
  35.9 126.7 %all-gather.20.cloned.1.call-start = ((), (), s32[]{:S(2)}) async-start(), calls=%async_computation.10 | async-start | bytes 2785280 | tf_op jit(solution)/shard_map/all_gather | solution.py:142
  97.3 103.9 %all-gather.22.cloned.1.call-start = ((), (), s32[]{:S(2)}) async-start(), calls=%async_computation.11 | async-start | bytes 2785280 | tf_op jit(solution)/shard_map/all_gather | solution.py:145
  100.2 174.0 %all-gather.28.cloned.1.call-start = ((), (), s32[]{:S(2)}) async-start(), calls=%async_computation.14 | async-start | bytes 11489280 | tf_op jit(solution)/shard_map/all_gather | solution.py:123
  114.2 208.3 %all-gather.18.cloned.1.call-start = ((), (), s32[]{:S(2)}) async-start(), calls=%async_computation.7 | async-start | bytes 10340352 | tf_op jit(solution)/shard_map/all_gather | solution.py:123
  128.4 406.3 %reduce-scatter.26.cloned.1.call-start = ((), (), s32[]{:S(2)}) async-start(), calls=%async_computation.9 | async-start | bytes 5570560 | tf_op jit(solution)/shard_map/reduce_scatter | solution.py:233
  486.1 99.7 %reduce-scatter.24.cloned.1.call-start = ((), (), s32[]{:S(2)}) async-start(), calls=%async_computation.8 | async-start | bytes 5570560 | tf_op jit(solution)/shard_map/reduce_scatter | solution.py:232
  486.9 595.8 %reduce-scatter.36.cloned.1.call-start = ((), (), s32[]{:S(2)}) async-start(), calls=%async_computation.19 | async-start | bytes 20680704
  500.8 588.3 %reduce-scatter.30.cloned.1.call-start = ((), (), s32[]{:S(2)}) async-start(), calls=%async_computation.16 | async-start | bytes 696320
  898.9 21.8 %collective-permute-start.13 = (f32[48,1088]{1,0:T(8,128)}, f32[48,1088]{1,0:T(8,128)}, u32[]{:S(2)}, u32[]{:S(2)}) collective-permute-start(f32[48,1088]{1,0:T(8,128)} %get-tuple-element.200), channel_id=1, source_target_pairs={{0,36},{4,40},{8,44},{12,48},{16,52},{20,56},{24,60},{28,64},{32,6... | collective-permute-start | bytes 626696
  900.8 23.8 %collective-permute-start.12 = (f32[48,1088]{1,0:T(8,128)}, f32[48,1088]{1,0:T(8,128)}, u32[]{:S(2)}, u32[]{:S(2)}) collective-permute-start(f32[48,1088]{1,0:T(8,128)} %get-tuple-element.200), channel_id=1, source_target_pairs={{0,32},{4,36},{8,40},{12,44},{16,48},{20,52},{24,56},{28,60},{32,6... | collective-permute-start | bytes 626696
  905.9 24.9 %collective-permute-start.11 = (f32[48,1088]{1,0:T(8,128)}, f32[48,1088]{1,0:T(8,128)}, u32[]{:S(2)}, u32[]{:S(2)}) collective-permute-start(f32[48,1088]{1,0:T(8,128)} %get-tuple-element.200), channel_id=1, source_target_pairs={{0,28},{4,32},{8,36},{12,40},{16,44},{20,48},{24,52},{28,56},{32,6... | collective-permute-start | bytes 626696
  913.1 20.4 %collective-permute-start.10 = (f32[48,1088]{1,0:T(8,128)}, f32[48,1088]{1,0:T(8,128)}, u32[]{:S(2)}, u32[]{:S(2)}) collective-permute-start(f32[48,1088]{1,0:T(8,128)} %get-tuple-element.200), channel_id=1, source_target_pairs={{0,24},{4,28},{8,32},{12,36},{16,40},{20,44},{24,48},{28,52},{32,5... | collective-permute-start | bytes 626696
  918.5 17.8 %collective-permute-start.9 = (f32[48,1088]{1,0:T(8,128)}, f32[48,1088]{1,0:T(8,128)}, u32[]{:S(2)}, u32[]{:S(2)}) collective-permute-start(f32[48,1088]{1,0:T(8,128)} %get-tuple-element.200), channel_id=1, source_target_pairs={{0,20},{4,24},{8,28},{12,32},{16,36},{20,40},{24,44},{28,48},{32,5... | collective-permute-start | bytes 626696
  920.6 18.5 %collective-permute-start.8 = (f32[48,1088]{1,0:T(8,128)}, f32[48,1088]{1,0:T(8,128)}, u32[]{:S(2)}, u32[]{:S(2)}) collective-permute-start(f32[48,1088]{1,0:T(8,128)} %get-tuple-element.200), channel_id=1, source_target_pairs={{0,16},{4,20},{8,24},{12,28},{16,32},{20,36},{24,40},{28,44},{32,4... | collective-permute-start | bytes 626696
  924.7 18.2 %collective-permute-start.7 = (f32[48,1088]{1,0:T(8,128)}, f32[48,1088]{1,0:T(8,128)}, u32[]{:S(2)}, u32[]{:S(2)}) collective-permute-start(f32[48,1088]{1,0:T(8,128)} %get-tuple-element.200), channel_id=1, source_target_pairs={{0,12},{4,16},{8,20},{12,24},{16,28},{20,32},{24,36},{28,40},{32,4... | collective-permute-start | bytes 626696
  930.8 14.7 %collective-permute-start.6 = (f32[48,1088]{1,0:T(8,128)}, f32[48,1088]{1,0:T(8,128)}, u32[]{:S(2)}, u32[]{:S(2)}) collective-permute-start(f32[48,1088]{1,0:T(8,128)} %get-tuple-element.200), channel_id=1, source_target_pairs={{0,8},{4,12},{8,16},{12,20},{16,24},{20,28},{24,32},{28,36},{32,40... | collective-permute-start | bytes 626696
  933.5 16.7 %collective-permute-start.5 = (f32[48,1088]{1,0:T(8,128)}, f32[48,1088]{1,0:T(8,128)}, u32[]{:S(2)}, u32[]{:S(2)}) collective-permute-start(f32[48,1088]{1,0:T(8,128)} %get-tuple-element.200), channel_id=1, source_target_pairs={{0,4},{4,8},{8,12},{12,16},{16,20},{20,24},{24,28},{28,32},{32,36}... | collective-permute-start | bytes 626696
  936.3 53.2 %collective-permute-start.3 = (f32[40,3264]{1,0:T(8,128)}, f32[40,3264]{1,0:T(8,128)}, u32[]{:S(2)}, u32[]{:S(2)}) collective-permute-start(f32[40,3264]{1,0:T(8,128)} %get-tuple-element.199), channel_id=1, source_target_pairs={{0,16},{4,20},{8,24},{12,28},{16,32},{20,36},{24,40},{28,44},{32,4... | collective-permute-start | bytes 1566728
  939.1 52.5 %collective-permute-start.2 = (f32[40,3264]{1,0:T(8,128)}, f32[40,3264]{1,0:T(8,128)}, u32[]{:S(2)}, u32[]{:S(2)}) collective-permute-start(f32[40,3264]{1,0:T(8,128)} %get-tuple-element.199), channel_id=1, source_target_pairs={{0,12},{4,16},{8,20},{12,24},{16,28},{20,32},{24,36},{28,40},{32,4... | collective-permute-start | bytes 1566728
  942.8 55.3 %collective-permute-start.1 = (f32[40,3264]{1,0:T(8,128)}, f32[40,3264]{1,0:T(8,128)}, u32[]{:S(2)}, u32[]{:S(2)}) collective-permute-start(f32[40,3264]{1,0:T(8,128)} %get-tuple-element.199), channel_id=1, source_target_pairs={{0,8},{4,12},{8,16},{12,20},{16,24},{20,28},{24,32},{28,36},{32,40... | collective-permute-start | bytes 1566728
  945.6 56.5 %collective-permute-start = (f32[40,3264]{1,0:T(8,128)}, f32[40,3264]{1,0:T(8,128)}, u32[]{:S(2)}, u32[]{:S(2)}) collective-permute-start(f32[40,3264]{1,0:T(8,128)} %get-tuple-element.199), channel_id=1, source_target_pairs={{0,4},{4,8},{8,12},{12,16},{16,20},{20,24},{24,28},{28,32},{32,36}... | collective-permute-start | bytes 1566728
  950.2 34.3 %collective-permute-start.4 = (f32[26,3264]{1,0:T(8,128)}, f32[26,3264]{1,0:T(8,128)}, u32[]{:S(2)}, u32[]{:S(2)}) collective-permute-start(f32[26,3264]{1,0:T(8,128)} %slice.65), channel_id=1, source_target_pairs={{0,20},{4,24},{8,28},{12,32},{16,36},{20,40},{24,44},{28,48},{32,5... | collective-permute-start | bytes 1018376
  983.4 107.3 %reduce-scatter.28.cloned.1.call-start = ((), (), s32[]{:S(2)}) async-start(), calls=%async_computation.15 | async-start | bytes 2088960
  984.5 61.4 %collective-permute-start.18 = (f32[40,4352]{1,0:T(8,128)S(1)}, f32[40,4352]{1,0:T(8,128)}, u32[]{:S(2)}, u32[]{:S(2)}) collective-permute-start(f32[40,4352]{1,0:T(8,128)S(1)} %get-tuple-element.201), channel_id=1, source_target_pairs={{0,16},{4,20},{8,24},{12,28},{16,32},{20,36},{24,40},{28,44},{32,4... | collective-permute-start | bytes 2088968
  989.4 56.4 %collective-permute-start.17 = (f32[40,4352]{1,0:T(8,128)S(1)}, f32[40,4352]{1,0:T(8,128)}, u32[]{:S(2)}, u32[]{:S(2)}) collective-permute-start(f32[40,4352]{1,0:T(8,128)S(1)} %get-tuple-element.201), channel_id=1, source_target_pairs={{0,12},{4,16},{8,20},{12,24},{16,28},{20,32},{24,36},{28,40},{32,4... | collective-permute-start | bytes 2088968
  991.6 54.3 %collective-permute-start.16 = (f32[40,4352]{1,0:T(8,128)S(1)}, f32[40,4352]{1,0:T(8,128)}, u32[]{:S(2)}, u32[]{:S(2)}) collective-permute-start(f32[40,4352]{1,0:T(8,128)S(1)} %get-tuple-element.201), channel_id=1, source_target_pairs={{0,8},{4,12},{8,16},{12,20},{16,24},{20,28},{24,32},{28,36},{32,40... | collective-permute-start | bytes 2088968
  998.2 47.7 %collective-permute-start.15 = (f32[40,4352]{1,0:T(8,128)S(1)}, f32[40,4352]{1,0:T(8,128)}, u32[]{:S(2)}, u32[]{:S(2)}) collective-permute-start(f32[40,4352]{1,0:T(8,128)S(1)} %get-tuple-element.201), channel_id=1, source_target_pairs={{0,4},{4,8},{8,12},{12,16},{16,20},{20,24},{24,28},{28,32},{32,36}... | collective-permute-start | bytes 2088968
  1002.1 43.7 %collective-permute-start.19 = (f32[26,4352]{1,0:T(8,128)}, f32[26,4352]{1,0:T(8,128)}, u32[]{:S(2)}, u32[]{:S(2)}) collective-permute-start(f32[26,4352]{1,0:T(8,128)} %slice.67), channel_id=1, source_target_pairs={{0,20},{4,24},{8,28},{12,32},{16,36},{20,40},{24,44},{28,48},{32,5... | collective-permute-start | bytes 1357832
  1039.8 81.1 %reduce-scatter.32.cloned.1.call-start = ((), (), s32[]{:S(2)}) async-start(), calls=%async_computation.17 | async-start | bytes 2785280
  1075.6 71.2 %reduce-scatter.34.cloned.1.call-start = ((), (), s32[]{:S(2)}) async-start(), calls=%async_computation.18 | async-start | bytes 1392640
  (38 other events, 1501.7 us)
Sparse Core Ops, SparseCore 0:
  22.3 55.7 all-gather.23
  80.9 44.5 all-gather.25
  127.8 34.7 all-gather.19
  164.7 36.5 all-gather.21
  203.4 60.4 all-gather.27
  266.1 56.3 all-gather.17
  486.3 48.3 reduce-scatter.25
  537.1 48.6 reduce-scatter.23
  589.8 317.9 reduce-scatter.35
  983.5 24.9 reduce-scatter.29
  1040.0 26.5 reduce-scatter.27
  1075.8 45.1 reduce-scatter.31
  1123.4 23.4 reduce-scatter.33
where the time goes:
time: 1250 us; the launch traced here: 1240 us
  blocking collectives  454 us (36%)
  matrix products  265 us (21%)
  waiting for transfers between devices  225 us (18%)
  local copies, waits for them, and re-layouts  156 us (12%)
  starting transfers between devices  89.6 us (7%)
  other arithmetic  28.5 us (2%)
  between operations  21.4 us (2%)
    unnamed x1, blocking collectives  302 us
    unnamed x100, local copies, waits for them, and re-layouts  119 us
    dot_general x38, matrix products, contract_first(): lax.dot_general(left_side, right_side, (((0,), (0,)), ((), ())), preferre...  96.2 us
    dot_general x55, matrix products, contract_last(): lax.dot_general(left_side, right_side, (((1,), (1,)), ((), ())), preferre...  94.3 us
    unnamed x25, starting transfers between devices  88.8 us
    psum x1, blocking collectives, body(): lax.psum(local_sq, ('dp', 'ctx')) + jnp.sum(vector_total * vector_total)  65.8 us
    unnamed x38, waiting for transfers between devices  59.7 us
    reduce_scatter x1, waiting for transfers between devices, body(): lax.psum_scatter(from_heads(d_key_h, full_len), 'ctx', scatter_dimension=...  49 us
  transfers between devices with their start and end apart: 33, of which 11 were waited for; matrix products, arithmetic and copies ran while one was open for 46% of the time, Pallas kernels for 0%

commit v1 on v0

v1 whole, which is shorter than its diff:
```python
import jax
import jax.numpy as jnp
from jax import lax
from jax.experimental import pallas as pl
from jax.experimental.pallas import tpu as pltpu
from jax.sharding import PartitionSpec as P

HEADS = 17
HEAD_DIM = 64
SLOTS = 5
GROUP = 4 * HEAD_DIM
SPAN = SLOTS * HEAD_DIM
STEP = 10

NORM_EPS = 1e-05
ADAM_EPS = 1e-08
BETA_FIRST = 0.9
BETA_SECOND = 0.999
CLIP_LIMIT = 1.0
GELU_SCALE = 0.7978845608
GELU_CUBIC = 0.044715
MASK_FILL = -1e30
LEARN_RATES = (0.05, 0.5, 0.1, 0.03, 1.0)
WEIGHT_DECAYS = (0.1, 0.1, 0.1, 0.1, 0.0)

LOW = jnp.bfloat16
FULL = jnp.float32
RING = 4
CORES = 2


def layer_norm(inputs, gain_col, shift_col):
    centre = inputs - jnp.mean(inputs, axis=-1, keepdims=True)
    spread = jnp.mean(centre * centre, axis=-1, keepdims=True)
    return centre * lax.rsqrt(spread + NORM_EPS) * gain_col + shift_col


def gelu(inputs):
    inner = GELU_SCALE * (inputs + GELU_CUBIC * inputs * inputs * inputs)
    return 0.5 * inputs * (1.0 + jnp.tanh(inner))


def adam_step(weight, moment, square, gradient, rate, decay):
    first = BETA_FIRST * moment + (1.0 - BETA_FIRST) * gradient
    second = BETA_SECOND * square + (1.0 - BETA_SECOND) * gradient * gradient
    first_hat = first / (1.0 - BETA_FIRST**STEP)
    second_hat = second / (1.0 - BETA_SECOND**STEP)
    updated = weight - rate * (first_hat / (jnp.sqrt(second_hat) + ADAM_EPS) + decay * weight)
    return (first, second, updated)


def dot(left, right):
    return jnp.dot(left, right, preferred_element_type=FULL)


def dot_last(left, right):
    return lax.dot_general(left, right, (((1,), (1,)), ((), ())), preferred_element_type=FULL)


def dot_first(left, right):
    return lax.dot_general(left, right, (((0,), (0,)), ((), ())), preferred_element_type=FULL)


def block_at(rank, index):
    return lax.rem(index + RING - rank, RING)


def bias_of(pos_row, query_block, key_block, length):
    keys = key_block * length + lax.broadcasted_iota(jnp.int32, (length, length), 0)
    queries = query_block * length + lax.broadcasted_iota(jnp.int32, (length, length), 1)
    allowed = (keys <= queries) & (keys >= queries - pos_row)
    return jnp.where(allowed, 0.0, MASK_FILL)


def head_cols(part, slot):
    first = part * SPAN + slot * HEAD_DIM
    return slice(first, first + HEAD_DIM)


def attend_forward(rank_ref, pos_ref, qkv_ref, heads_ref, lse_ref, turned_ref):
    rank = rank_ref[0]
    length = qkv_ref.shape[1]
    scale = HEAD_DIM ** (-0.5)
    for key_block in range(RING):
        at = block_at(rank, key_block)
        turned_ref[key_block] = qkv_ref[at, :, 2 * SPAN : 3 * SPAN].T
    for query_block in range(RING):
        at = block_at(rank, query_block)
        pos_row = pos_ref[at]
        biases = [bias_of(pos_row, query_block, k, length) for k in range(query_block + 1)]
        columns = []
        for slot in range(SLOTS):
            query = qkv_ref[at, :, head_cols(0, slot)] * jnp.asarray(scale, LOW)
            scores = [
                dot_last(qkv_ref[block_at(rank, k), :, head_cols(1, slot)], query) + biases[k]
                for k in range(query_block + 1)
            ]
            peak = jnp.max(scores[0], axis=0, keepdims=True)
            for part in scores[1:]:
                peak = jnp.maximum(peak, jnp.max(part, axis=0, keepdims=True))
            terms = [jnp.exp(part - peak) for part in scores]
            total = jnp.sum(terms[0], axis=0, keepdims=True)
            for part in terms[1:]:
                total = total + jnp.sum(part, axis=0, keepdims=True)
            inverse = 1.0 / total
            result = None
            for k in range(query_block + 1):
                value = turned_ref[k, slot * HEAD_DIM : (slot + 1) * HEAD_DIM, :]
                term = dot(value, (terms[k] * inverse).astype(LOW))
                result = term if result is None else result + term
            columns.append(result)
            lse_ref[at, slot : slot + 1, :] = peak + jnp.log(total)
        heads_ref[at] = jnp.concatenate(columns, axis=0).T.astype(LOW)


def attend_backward(
    rank_ref, pos_ref, qkv_ref, grad_ref, lse_ref, out_ref, turned_ref, bias_ref
):
    rank = rank_ref[0]
    length = qkv_ref.shape[1]
    scale = HEAD_DIM ** (-0.5)
    pairs = [(q, k) for q in range(RING) for k in range(q + 1)]
    for key_block in range(RING):
        turned_ref[key_block] = qkv_ref[block_at(rank, key_block), :, SPAN : 2 * SPAN].T
    for number, (q, k) in enumerate(pairs):
        bias_ref[number] = bias_of(pos_ref[block_at(rank, q)], q, k, length)
    for slot in range(SLOTS):
        rows = slice(slot * HEAD_DIM, (slot + 1) * HEAD_DIM)
        keys = [qkv_ref[block_at(rank, k), :, head_cols(1, slot)] for k in range(RING)]
        values = [qkv_ref[block_at(rank, k), :, head_cols(2, slot)] for k in range(RING)]
        d_keys = [None] * RING
        d_values = [None] * RING
        if slot == SLOTS - 1:
            keep = jnp.where(rank == RING - 1, 1.0, 0.0)
        else:
            keep = None

        def finish(item):
            return (item if keep is None else item * keep).astype(LOW)

        for q in range(RING):
            at = block_at(rank, q)
            query = qkv_ref[at, :, head_cols(0, slot)] * jnp.asarray(scale, LOW)
            grad = grad_ref[at, :, rows]
            lse = lse_ref[at, slot : slot + 1, :]
            probs = []
            d_probs = []
            inner = None
            for k in range(q + 1):
                score = dot_last(keys[k], query) + bias_ref[pairs.index((q, k))]
                prob = jnp.exp(score - lse)
                d_prob = dot_last(values[k], grad)
                term = jnp.sum(prob * d_prob, axis=0, keepdims=True)
                inner = term if inner is None else inner + term
                probs.append(prob)
                d_probs.append(d_prob)
            d_query = None
            for k in range(q + 1):
                d_score = (probs[k] * (d_probs[k] - inner)).astype(LOW)
                d_key = dot(d_score, query)
                d_value = dot(probs[k].astype(LOW), grad)
                term = dot(turned_ref[k, rows, :], d_score)
                d_keys[k] = d_key if d_keys[k] is None else d_keys[k] + d_key
                d_values[k] = d_value if d_values[k] is None else d_values[k] + d_value
                d_query = term if d_query is None else d_query + term
            out_ref[at, :, head_cols(0, slot)] = finish(d_query.T * scale)
        for k in range(RING):
            at = block_at(rank, k)
            out_ref[at, :, head_cols(1, slot)] = finish(d_keys[k])
            out_ref[at, :, head_cols(2, slot)] = finish(d_values[k])


VMEM_SPEC = pl.BlockSpec(memory_space=pltpu.VMEM)
SMEM_SPEC = pl.BlockSpec(memory_space=pltpu.SMEM)
KERNEL_PARAMS = pltpu.CompilerParams(vmem_limit_bytes=48 * 1024 * 1024)


def run_forward(rank, pos, qkv):
    blocks, length, unused = qkv.shape
    return pl.pallas_call(
        attend_forward,
        out_shape=(
            jax.ShapeDtypeStruct((blocks, length, SPAN), LOW),
            jax.ShapeDtypeStruct((blocks, 8, length), FULL),
        ),
        in_specs=[SMEM_SPEC, VMEM_SPEC, VMEM_SPEC],
        out_specs=(VMEM_SPEC, VMEM_SPEC),
        scratch_shapes=[pltpu.VMEM((blocks, SPAN, length), LOW)],
        compiler_params=KERNEL_PARAMS,
        cost_estimate=pl.CostEstimate(
            flops=2 * 2 * 10 * 256 * 256 * SPAN, bytes_accessed=4 << 20, transcendentals=3 << 20
        ),
    )(rank, pos, qkv)


def run_backward(rank, pos, qkv, grads, lse):
    blocks, length, width = qkv.shape
    return pl.pallas_call(
        attend_backward,
        out_shape=jax.ShapeDtypeStruct((blocks, length, width), LOW),
        in_specs=[SMEM_SPEC, VMEM_SPEC, VMEM_SPEC, VMEM_SPEC, VMEM_SPEC],
        out_specs=VMEM_SPEC,
        scratch_shapes=[
            pltpu.VMEM((blocks, SPAN, length), LOW),
            pltpu.VMEM((10, length, length), FULL),
        ],
        compiler_params=KERNEL_PARAMS,
        cost_estimate=pl.CostEstimate(
            flops=2 * 5 * 10 * 256 * 256 * SPAN, bytes_accessed=8 << 20, transcendentals=3 << 20
        ),
    )(rank, pos, qkv, grads, lse)


def ctx_shift(item, step):
    return lax.ppermute(item, "ctx", [(i, (i + step) % RING) for i in range(RING)])


def gather_relative(item):
    half = item.shape[0] // 2
    left = ctx_shift(item, 1)
    right = ctx_shift(item, 3)
    top = ctx_shift(left[:half], 1)
    bottom = ctx_shift(right[half:], 3)
    return jnp.concatenate([item, right, top, bottom, left], axis=0)


def gather_small(item):
    return jnp.stack([item, ctx_shift(item, 3), ctx_shift(item, 2), ctx_shift(item, 1)])


def to_global(relative, rank):
    doubled = jnp.concatenate([relative, relative[: RING - 1]], axis=0)
    return lax.dynamic_slice_in_dim(doubled, lax.rem(RING - rank, RING), RING, axis=0)


def exchange(pieces):
    return [pieces[0]] + [ctx_shift(pieces[RING - r], RING - r) for r in (1, 2, 3)]


def reduce_ctx(partial):
    length = partial.shape[0] // RING
    own = partial[:length]
    others = partial[length:].astype(LOW)
    arrived = [
        ctx_shift(others[(r - 1) * length : r * length], r).astype(FULL) for r in (1, 2, 3)
    ]
    return own + (arrived[0] + arrived[1] + arrived[2])


def dp_perm(dp_count, move):
    rows = dp_count // (RING * CORES)
    pairs = []
    for z in range(RING):
        for y in range(rows):
            for core in range(CORES):
                to_z, to_y, to_core = move(z, y, core, rows)
                pairs.append(((z * rows + y) * CORES + core, (to_z * rows + to_y) * CORES + to_core))
    return pairs


def reduce_dp(grad, rank_z, rank_y, rank_core, order):
    dp_count = grad.shape[0] * grad.shape[1] * grad.shape[2]
    other = lax.dynamic_index_in_dim(grad, 1 - rank_core, 2, keepdims=False).astype(LOW)
    own = lax.dynamic_index_in_dim(grad, rank_core, 2, keepdims=False)
    swap = dp_perm(dp_count, lambda z, y, core, rows: (z, y, 1 - core))
    total = own.astype(FULL) + lax.ppermute(other, "dp", swap).astype(FULL)
    for name in order:
        axis = 0 if (name == "z" or order[0] == "z") else 1
        size = total.shape[axis]
        at = rank_z if name == "z" else rank_y
        low = total.astype(LOW)
        result = lax.dynamic_index_in_dim(total, at, axis, keepdims=False)
        for step in range(1, size):
            piece = lax.dynamic_index_in_dim(low, lax.rem(at + step, size), axis, keepdims=False)
            if name == "z":
                perm = dp_perm(dp_count, lambda z, y, core, rows: ((z + step) % RING, y, core))
            else:
                perm = dp_perm(dp_count, lambda z, y, core, rows: (z, (y + step) % rows, core))
            result = result + lax.ppermute(piece, "dp", perm).astype(FULL)
        total = result
    return total


def sum_everywhere(item, dp_count):
    rows = dp_count // (RING * CORES)
    swap = dp_perm(dp_count, lambda z, y, core, rows: (z, y, 1 - core))
    item = item + lax.ppermute(item, "dp", swap)
    for name in ("y", "z", "x"):
        parts = [item]
        for step in (1, 2, 3):
            if name == "x":
                perm = [(i, i ^ step) for i in range(RING)]
                parts.append(lax.ppermute(item, "ctx", perm))
            elif name == "z":
                perm = dp_perm(dp_count, lambda z, y, core, rows: (z ^ step, y, core))
                parts.append(lax.ppermute(item, "dp", perm))
            elif rows == RING:
                perm = dp_perm(dp_count, lambda z, y, core, rows: (z, y ^ step, core))
                parts.append(lax.ppermute(item, "dp", perm))
        if len(parts) == RING:
            item = (parts[0] + parts[1]) + (parts[2] + parts[3])
    return item


def swap_planes(item, dp_count):
    inner = dp_count // RING
    pairs = [
        ((z * inner + rest) * RING + x, (x * inner + rest) * RING + z)
        for z in range(RING)
        for rest in range(inner)
        for x in range(RING)
    ]
    return lax.ppermute(item, ("dp", "ctx"), pairs)


def body(
    tokens,
    cotangent,
    positions,
    w_qkv,
    w_out,
    w_up,
    w_down,
    vectors,
    moment_qkv,
    square_qkv,
    moment_out,
    square_out,
    moment_up,
    square_up,
    moment_down,
    square_down,
    moment_vec,
    square_vec,
):
    unused, local_len, width = tokens.shape
    dp_count = lax.axis_size("dp")
    rows_y = dp_count // (RING * CORES)
    rank = lax.axis_index("ctx")
    dp_rank = lax.axis_index("dp")
    rank_core = lax.rem(dp_rank, CORES)
    rank_y = lax.rem(lax.div(dp_rank, CORES), rows_y)
    rank_z = lax.div(dp_rank, CORES * rows_y)
    row_size = w_qkv.shape[0]
    full_len = local_len * RING

    shard_cols = jnp.concatenate(
        [w_qkv.astype(LOW), w_out.astype(LOW), vectors.astype(LOW)], axis=1
    )
    gathered = to_global(gather_small(shard_cols), rank)
    qkv_size, out_size = w_qkv.shape[1], w_out.shape[1]
    qkv_rows = jnp.concatenate([gathered[s, :, :qkv_size] for s in range(RING)], axis=1)
    out_rows = jnp.concatenate(
        [gathered[s, :, qkv_size : qkv_size + out_size] for s in range(RING)], axis=1
    )
    vec_rows = jnp.concatenate([gathered[s, :, qkv_size + out_size :] for s in range(RING)], axis=1)
    head_start = rank * GROUP
    qkv_own = [
        lax.dynamic_slice_in_dim(qkv_rows[:, part * width : (part + 1) * width], head_start, SPAN, 1)
        for part in range(3)
    ]
    first_all = lax.all_gather(
        jnp.concatenate(qkv_own + [vec_rows], axis=1), "dp", axis=0, tiled=True
    )
    down_swapped = swap_planes(w_down.astype(LOW), dp_count)
    down_shape = down_swapped.shape
    second_all = lax.all_gather(
        jnp.concatenate(
            [out_rows, w_up.astype(LOW), down_swapped.reshape(row_size, width)], axis=1
        ),
        "dp",
        axis=0,
        tiled=False,
    )
    qkv_low = first_all[:, : 3 * SPAN]
    vec_full = first_all[:, 3 * SPAN :].astype(FULL)
    out_low = second_all[:, :, :width].reshape(width, width)
    up_low = second_all[:, :, width : 2 * width].reshape(width, width)
    down_low = (
        second_all[:, :, 2 * width :]
        .reshape(RING, dp_count // RING * down_shape[0], down_shape[1])
        .transpose(1, 0, 2)
        .reshape(width, width)
    )

    token_low = tokens.reshape(local_len, width)
    cot_low = cotangent.reshape(local_len, width)
    token_seq = gather_relative(token_low)
    pos_seq = gather_small(positions)
    cot_seq = gather_relative(cot_low)
    rank_arg = rank.astype(jnp.int32).reshape(1)

    a_one = layer_norm(token_seq.astype(FULL), vec_full[:, 0], vec_full[:, 1]).astype(LOW)
    q_bias = lax.dynamic_slice_in_dim(vec_full[:, 2], head_start, SPAN, 0)
    v_bias = lax.dynamic_slice_in_dim(vec_full[:, 3], head_start, SPAN, 0)
    qkv_bias = jnp.concatenate([q_bias, jnp.zeros_like(q_bias), v_bias])
    qkv_seq = (dot(a_one, qkv_low) + qkv_bias).astype(LOW)
    qkv_blocks = qkv_seq.reshape(RING, local_len, 3 * SPAN)
    heads_blocks, lse = run_forward(rank_arg, pos_seq, qkv_blocks)

    came = exchange([heads_blocks[r] for r in range(RING)])
    by_group = to_global(jnp.stack(came), rank)
    heads_low = jnp.concatenate(
        [by_group[s, :, :GROUP] for s in range(RING - 1)] + [by_group[RING - 1]], axis=1
    )
    inputs = token_low.astype(FULL)
    mixed = inputs + (dot(heads_low, out_low) + vec_full[:, 4])
    a_two = layer_norm(mixed, vec_full[:, 5], vec_full[:, 6]).astype(LOW)
    a_two_seq = gather_relative(a_two)
    up_bias = lax.dynamic_index_in_dim(vec_full, 7 + rank, 1, keepdims=False)
    d_act = dot_last(cot_seq, down_low)
    pre_act = dot(a_two_seq, up_low) + up_bias
    act, gelu_pull = jax.vjp(gelu, pre_act)
    act_low = act.astype(LOW)
    d_pre = gelu_pull(d_act)[0].astype(LOW)
    d_two = reduce_ctx(dot_last(d_pre, up_low))
    down_sum = reduce_ctx(dot(act_low, down_low))
    outputs = (mixed + (down_sum + vec_full[:, 11])).astype(LOW).reshape(tokens.shape)

    unused, second_pull = jax.vjp(layer_norm, mixed, vec_full[:, 5], vec_full[:, 6])
    d_mixed_part, d_gain_two, d_shift_two = second_pull(d_two)
    cot_full = cot_low.astype(FULL)
    d_mixed = cot_full + d_mixed_part
    d_branch = d_mixed.astype(LOW)
    d_heads = dot_last(d_branch, out_low).astype(LOW)
    pieces = [
        lax.dynamic_slice_in_dim(d_heads, lax.rem(rank + r, RING) * GROUP, SPAN, 1)
        for r in range(RING)
    ]
    d_heads_blocks = jnp.stack(exchange(pieces))
    d_qkv_blocks = run_backward(rank_arg, pos_seq, qkv_blocks, d_heads_blocks, lse)
    d_qkv = d_qkv_blocks.reshape(full_len, 3 * SPAN)

    def summed(grad, order):
        return reduce_dp(grad, rank_z, rank_y, rank_core, order)

    lead = (RING, rows_y, CORES)
    grad_up = summed(
        dot_first(a_two_seq, d_pre).astype(LOW).reshape(lead + (row_size, width)), ("y", "z")
    )
    grad_down_part = (
        dot_first(act_low, cot_seq)
        .astype(LOW)
        .reshape(rows_y, CORES, down_shape[0], RING, down_shape[1])
        .transpose(3, 0, 1, 2, 4)
    )
    grad_down = swap_planes(summed(grad_down_part, ("z", "y")), dp_count)
    grad_out_part = dot_first(heads_low, d_branch).astype(LOW)
    out_pieces = [
        lax.dynamic_slice_in_dim(grad_out_part, lax.rem(rank + r, RING) * out_size, out_size, 1)
        for r in range(RING)
    ]
    out_came = exchange(out_pieces)
    grad_out_cols = (
        (out_came[0].astype(FULL) + out_came[1].astype(FULL))
        + (out_came[2].astype(FULL) + out_came[3].astype(FULL))
    ).astype(LOW)
    grad_out = summed(grad_out_cols.reshape(lead + (row_size, out_size)), ("y", "z"))
    grad_qkv_part = dot_first(a_one, d_qkv).astype(LOW).reshape(lead + (row_size, 3 * SPAN))
    split = 512
    grad_qkv_own = jnp.concatenate(
        [
            summed(grad_qkv_part[..., :split], ("y", "z")),
            summed(grad_qkv_part[..., split:], ("z", "y")),
        ],
        axis=1,
    )
    d_one = reduce_ctx(dot_last(d_qkv, qkv_low))
    unused, first_pull = jax.vjp(layer_norm, inputs, vec_full[:, 0], vec_full[:, 1])
    d_input_part, d_gain_one, d_shift_one = first_pull(d_one)
    d_tokens = (d_mixed + d_input_part).reshape(tokens.shape)

    d_qkv_sums = jnp.sum(d_qkv.astype(FULL), axis=0)
    empty = jnp.zeros((width,), FULL)
    d_pre_sums = jnp.sum(d_pre.astype(FULL), axis=0)
    vec_terms = jnp.stack(
        [
            d_gain_one,
            d_shift_one,
            lax.dynamic_update_slice(empty, d_qkv_sums[:SPAN], (head_start,)),
            lax.dynamic_update_slice(empty, d_qkv_sums[2 * SPAN :], (head_start,)),
            jnp.sum(d_branch.astype(FULL), axis=0),
            d_gain_two,
            d_shift_two,
        ]
        + [jnp.where(rank == c, d_pre_sums, 0.0) for c in range(RING)]
        + [jnp.sum(cot_full, axis=0)],
        axis=0,
    )
    local_sq = (
        jnp.sum(grad_qkv_own * grad_qkv_own)
        + jnp.sum(grad_out * grad_out)
        + jnp.sum(grad_up * grad_up)
        + jnp.sum(grad_down * grad_down)
    )
    vec_count = vec_terms.shape[0]
    payload = jnp.concatenate(
        [
            vec_terms,
            jnp.where(lax.broadcasted_iota(jnp.int32, (4, width), 1) == 0, local_sq, 0.0)
            * jnp.where(lax.broadcasted_iota(jnp.int32, (4, width), 0) == 0, 1.0, 0.0),
        ],
        axis=0,
    )
    payload = sum_everywhere(payload, dp_count)
    vec_total = payload[:vec_count]
    total_sq = payload[vec_count, 0] + jnp.sum(vec_total * vec_total)
    grad_norm = jnp.sqrt(total_sq)
    clip_factor = CLIP_LIMIT / jnp.maximum(grad_norm, CLIP_LIMIT)

    col_size = vec_count // RING
    grad_vec = lax.dynamic_slice(
        vec_total, (rank * col_size, dp_rank * row_size), (col_size, row_size)
    ).T
    qkv_groups = to_global(gather_small(grad_qkv_own), rank)
    grad_qkv_rows = jnp.concatenate(
        [
            qkv_groups[s, :, part * SPAN : part * SPAN + (SPAN if s == RING - 1 else GROUP)]
            for part in range(3)
            for s in range(RING)
        ],
        axis=1,
    )
    grad_qkv = lax.dynamic_slice_in_dim(grad_qkv_rows, rank * qkv_size, qkv_size, 1)

    first_qkv, second_qkv, updated_qkv = adam_step(
        w_qkv, moment_qkv, square_qkv, grad_qkv * clip_factor, LEARN_RATES[0], WEIGHT_DECAYS[0]
    )
    first_out, second_out, updated_out = adam_step(
        w_out, moment_out, square_out, grad_out * clip_factor, LEARN_RATES[1], WEIGHT_DECAYS[1]
    )
    first_up, second_up, updated_up = adam_step(
        w_up, moment_up, square_up, grad_up * clip_factor, LEARN_RATES[2], WEIGHT_DECAYS[2]
    )
    first_down, second_down, updated_down = adam_step(
        w_down, moment_down, square_down, grad_down * clip_factor, LEARN_RATES[3], WEIGHT_DECAYS[3]
    )
    first_vec, second_vec, updated_vec = adam_step(
        vectors, moment_vec, square_vec, grad_vec * clip_factor, LEARN_RATES[4], WEIGHT_DECAYS[4]
    )
    return (
        outputs,
        d_tokens,
        grad_norm,
        first_qkv,
        second_qkv,
        updated_qkv,
        first_out,
        second_out,
        updated_out,
        first_up,
        second_up,
        updated_up,
        first_down,
        second_down,
        updated_down,
        first_vec,
        second_vec,
        updated_vec,
    )


def solution(mesh):
    token_spec = P("dp", "ctx", None)
    flat_spec = P("dp", "ctx")
    return jax.shard_map(
        body,
        mesh=mesh,
        in_specs=(token_spec, token_spec) + (flat_spec,) * 16,
        out_specs=(token_spec, token_spec, P()) + (flat_spec,) * 15,
        check_vma=False,
    )
```

time: 1250 us -> 552 us (0.44)
  blocking collectives: 454 us -> 0 us
  matrix products: 265 us -> 52 us
  waiting for transfers between devices: 225 us -> 130 us
  starting transfers between devices: 89.6 us -> 145 us
  local copies, waits for them, and re-layouts: 156 us -> 130 us
  Pallas kernels: 0 us -> 22.8 us
  other arithmetic: 28.5 us -> 43.4 us
    unnamed x1 -> x0, blocking collectives: 302 us -> none
    dot_general x131 -> x12, matrix products: 265 us -> 52 us  [the longest x4 18.8 us: dot_last(): lax.dot_general(left, right, (((1,), (1,)), ((), ())), preferred_element_...]
    ppermute x0 -> x86, starting transfers between devices: none -> 145 us  [the longest x39 72.7 us: ctx_shift(): lax.ppermute(item, 'ctx', [(i, (i + step) % RING) for i in range(RING)])]
    ppermute x0 -> x86, waiting for transfers between devices: none -> 130 us  [the longest x39 101 us: ctx_shift(): lax.ppermute(item, 'ctx', [(i, (i + step) % RING) for i in range(RING)])]
    all_gather x6 -> x2, waiting for transfers between devices: 95 us -> 0.04 us  [the longest x1 0.02 us: body(): lax.all_gather(jnp.concatenate(qkv_own + [vec_rows], axis=1), 'dp', axis=...]
    unnamed x25 -> x0, starting transfers between devices: 88.8 us -> none
    unnamed x100 -> x131, local copies, waits for them, and re-layouts: 119 us -> 30.1 us
    all_gather x6 -> x0, blocking collectives: 86 us -> none  [the longest x1 26.1 us: body(): vec_piece = lax.all_gather(vec_cols, 'dp', axis=0, tiled=True)]
  transfers between devices with their start and end apart: 33 -> 88, of which waited for: 11 -> 35; matrix products, arithmetic and copies ran while one was open for 46% -> 28% of each run, Pallas kernels for 0% -> 4%
where the time goes in v1:
time: 552 us; the launch traced here: 544 us
  starting transfers between devices  145 us (26%)
  local copies, waits for them, and re-layouts  130 us (24%)
  waiting for transfers between devices  130 us (24%)
  matrix products  52 us (9%)
  other arithmetic  43.4 us (8%)
  Pallas kernels  22.8 us (4%)
  between operations  21 us (4%)
    ppermute x39, waiting for transfers between devices, ctx_shift(): lax.ppermute(item, 'ctx', [(i, (i + step) % RING) for i in range(RING)])  101 us
    ppermute x39, starting transfers between devices, ctx_shift(): lax.ppermute(item, 'ctx', [(i, (i + step) % RING) for i in range(RING)])  72.7 us
    ppermute x30, starting transfers between devices, reduce_dp(): result = result + lax.ppermute(piece, 'dp', perm).astype(FULL)  49.7 us
    unnamed x131, local copies, waits for them, and re-layouts  30.1 us
    dot_general x4, matrix products, dot_last(): lax.dot_general(left, right, (((1,), (1,)), ((), ())), preferred_element_...  18.8 us
    ppermute x30, waiting for transfers between devices, reduce_dp(): result = result + lax.ppermute(piece, 'dp', perm).astype(FULL)  18.1 us
    dot_general x4, matrix products, dot(): return jnp.dot(left, right, preferred_element_type=FULL)  17.6 us
    dot_general x4, matrix products, dot_first(): lax.dot_general(left, right, (((0,), (0,)), ((), ())), preferred_element_...  15.6 us
  transfers between devices with their start and end apart: 88, of which 35 were waited for; matrix products, arithmetic and copies ran while one was open for 28% of the time, Pallas kernels for 4%

profile of v1, /device:TPU:0, one launch (start us, length us, event | category | flops | bytes accessed | tf_op | source)
XLA Modules:
  0.0 544.5 jit_solution(11207126791898762681)
XLA Ops:
  23.8 12.5 %collective-permute-start.3 = (bf16[256,1088]{0,1:T(8,128)(2,1)S(1)}, bf16[256,1088]{0,1:T(8,128)(2,1)}, u32[]{:S(2)}, u32[]{:S(2)}) collective-permute-start(bf16[256,1088]{0,1:T(8,128)(2,1)S(1)} %bitcast.341), channel_id=1, source_target_pairs={{0,3},{1,0},{2,1},{3,2},{4,7},{5,4},{6,5},{7,6},{8,11},{9,8},{10,9... | collective-permute-start | bytes 1671176 | tf_op jit(solution)/shard_map/ppermute | solution.py:215
  42.5 8.9 %collective-permute-done.4 = bf16[256,1088]{0,1:T(8,128)(2,1)S(1)} collective-permute-done((bf16[256,1088]{0,1:T(8,128)(2,1)S(1)}, bf16[256,1088]{0,1:T(8,128)(2,1)S(1)}, u32[]{:S(2)}, u32[]{:S(2)}) %collective-permute-start.4) | collective-permute-done | bytes 557088 | tf_op jit(solution)/shard_map/ppermute | solution.py:215
  59.2 12.7 %collective-permute-done.5 = bf16[128,1088]{0,1:T(8,128)(2,1)S(1)} collective-permute-done((bf16[128,1088]{0,1:T(8,128)(2,1)S(1)}, bf16[128,1088]{0,1:T(8,128)(2,1)S(1)}, u32[]{:S(2)}, u32[]{:S(2)}) %collective-permute-start.5) | collective-permute-done | bytes 278560 | tf_op jit(solution)/shard_map/ppermute | solution.py:215
  81.4 4.4 add_convert_fusion
  88.9 9.3 %shard_map.313 = (bf16[4,256,320]{2,1,0:T(8,128)(2,1)S(1)}, f32[4,8,256]{2,1,0:T(8,128)S(1)}) custom-call(s32[1]{0:T(128)} %bitcast.1.rank_ref, s32[4,1,256]{2,1,0:T(1,128)S(1)} %pad_add_fusion.pos_ref, bf16[4,256,960]{2,1,0:T(8,128)(2,1)S(1)} %bitcast.337), custom_call_target="tpu_custom_call" | custom-call | flops 838860800 | bytes 4194304 | tf_op jit(solution)/shard_map/pallas_call | solution.py:180
  108.8 6.0 %collective-permute-done.11 = bf16[256,320]{1,0:T(8,128)(2,1)S(1)} collective-permute-done((bf16[256,320]{1,0:T(8,128)(2,1)}, bf16[256,320]{1,0:T(8,128)(2,1)S(1)}, u32[]{:S(2)}, u32[]{:S(2)}) %collective-permute-start.11) | collective-permute-done | bytes 163872 | tf_op jit(solution)/shard_map/ppermute | solution.py:215
  123.2 7.0 %fusion.105 = (bf16[32,34,1088]{2,1,0:T(8,128)(2,1)}, bf16[32,34,1088]{2,1,0:T(8,128)(2,1)}, bf16[32,34,1088]{2,1,0:T(8,128)(2,1)}) fusion(bf16[32,34,3264]{2,1,0:T(8,128)(2,1)} %all-gather.8.cloned.1.call-done), kind=kLoop, calls=%fused_computation.332 | loop fusion | bytes 14204928 | tf_op jit(solution)/shard_map/slice | solution.py:378
  130.3 4.5 reshape.233
  148.0 6.5 %collective-permute-done.15 = bf16[256,1088]{0,1:T(8,128)(2,1)S(1)} collective-permute-done((bf16[256,1088]{0,1:T(8,128)(2,1)}, bf16[256,1088]{0,1:T(8,128)(2,1)S(1)}, u32[]{:S(2)}, u32[]{:S(2)}) %collective-permute-start.15) | collective-permute-done | bytes 557088 | tf_op jit(solution)/shard_map/ppermute | solution.py:215
  157.5 4.6 reshape.234
  162.0 7.0 %reshape.235 = bf16[4,1088,272]{2,1,0:T(8,128)(2,1)} reshape(bf16[32,34,1088]{2,1,0:T(8,128)(2,1)} %get-tuple-element.80) | data formatting | bytes 4734976 | tf_op jit(solution)/shard_map/reshape | solution.py:381
  169.0 4.6 copy.161
  184.3 4.8 convolution_add_fusion
  189.1 7.2 %convolution_convert_fusion.1 = bf16[1088,1088]{1,0:T(8,128)(2,1)} fusion(bf16[1024,1088]{0,1:T(8,128)(2,1)} %constant_dynamic-update-slice_fusion.10, f32[1024,1088]{0,1:T(8,128)S(1)} %convolution_add_fusion), kind=kOutput, calls=%fused_computation.1 | convolution fusion | flops 2435518464 | bytes 9052160 | tf_op jit(solution)/shard_map/dot_general | solution.py:61
  196.3 8.2 %convert_reduce_fusion.1 = (f32[1088]{0:T(1024)S(1)}, bf16[1024,1088]{0,1:T(8,128)(2,1)S(1)}) fusion(f32[1024,1088]{0,1:T(8,128)S(1)} %convolution_add_fusion, bf16[1024,1088]{0,1:T(8,128)(2,1)} %constant_dynamic-update-slice_fusion.10, bf16[1088,1088]{0,1:T(8,128)(2,1)S(1)} %bitcast.344), kind=kOutput, calls=%fused_computation.22 | convolution fusion | flops 2453273600 | bytes 11284736 | tf_op jit(solution)/shard_map/dot_general | solution.py:57
  204.5 5.4 fusion.113
  209.9 4.4 convolution_convert_fusion.2
  214.3 5.0 fusion.112
  219.3 7.3 %reshape.248 = bf16[4,2,136,4,272]{4,3,2,1,0:T(4,128)(2,1)} reshape(bf16[1088,1088]{1,0:T(8,128)(2,1)} %convolution_convert_fusion.1) | data formatting | bytes 4734976 | tf_op jit(solution)/shard_map/reshape | solution.py:444
  232.4 4.4 reshape.247
  248.6 7.9 %collective-permute-done.25 = bf16[256,1088]{0,1:T(8,128)(2,1)S(1)} collective-permute-done((bf16[256,1088]{0,1:T(8,128)(2,1)S(1)}, bf16[256,1088]{0,1:T(8,128)(2,1)S(1)}, u32[]{:S(2)}, u32[]{:S(2)}) %collective-permute-start.25) | collective-permute-done | bytes 557088 | tf_op jit(solution)/shard_map/ppermute | solution.py:215
  257.7 12.8 %collective-permute-done.26 = bf16[256,1088]{0,1:T(8,128)(2,1)S(1)} collective-permute-done((bf16[256,1088]{0,1:T(8,128)(2,1)S(1)}, bf16[256,1088]{0,1:T(8,128)(2,1)S(1)}, u32[]{:S(2)}, u32[]{:S(2)}) %collective-permute-start.26) | collective-permute-done | bytes 557088 | tf_op jit(solution)/shard_map/ppermute | solution.py:215
  275.0 7.5 %collective-permute-done.18 = bf16[256,1088]{0,1:T(8,128)(2,1)S(1)} collective-permute-done((bf16[256,1088]{0,1:T(8,128)(2,1)S(1)}, bf16[256,1088]{0,1:T(8,128)(2,1)S(1)}, u32[]{:S(2)}, u32[]{:S(2)}) %collective-permute-start.18) | collective-permute-done | bytes 557088 | tf_op jit(solution)/shard_map/ppermute | solution.py:215
  282.4 11.1 %collective-permute-done.19 = bf16[256,1088]{0,1:T(8,128)(2,1)S(1)} collective-permute-done((bf16[256,1088]{0,1:T(8,128)(2,1)S(1)}, bf16[256,1088]{0,1:T(8,128)(2,1)S(1)}, u32[]{:S(2)}, u32[]{:S(2)}) %collective-permute-start.19) | collective-permute-done | bytes 557088 | tf_op jit(solution)/shard_map/ppermute | solution.py:215
  317.6 13.4 %shard_map.314 = bf16[4,256,960]{2,1,0:T(8,128)(2,1)S(1)} custom-call(s32[1]{0:T(128)} %bitcast.1.rank_ref, s32[4,1,256]{2,1,0:T(1,128)S(1)} %pad_add_fusion.pos_ref, bf16[4,256,960]{2,1,0:T(8,128)(2,1)S(1)} %bitcast.338, bf16[4,256,320]{2,1,0:T(8,128)(2,1)S(1)} %pad_maximum_fusion.grad_ref, f32[4,8,256]{2,1,0:T(8,128)S(1)} %get-tuple-element.21.lse_ref), custom_call_target="tpu_custom_call" | custom-call | flops 2097152000 | bytes 8388608 | tf_op jit(solution)/shard_map/pallas_call | solution.py:198
  343.4 4.6 fusion.114
  377.5 5.7 %collective-permute-done.32 = bf16[256,1088]{0,1:T(8,128)(2,1)S(1)} collective-permute-done((bf16[256,1088]{0,1:T(8,128)(2,1)}, bf16[256,1088]{0,1:T(8,128)(2,1)S(1)}, u32[]{:S(2)}, u32[]{:S(2)}) %collective-permute-start.32) | collective-permute-done | bytes 557088 | tf_op jit(solution)/shard_map/ppermute | solution.py:215
  385.3 6.6 %collective-permute-done.33 = bf16[256,1088]{0,1:T(8,128)(2,1)S(1)} collective-permute-done((bf16[256,1088]{0,1:T(8,128)(2,1)S(1)}, bf16[256,1088]{0,1:T(8,128)(2,1)S(1)}, u32[]{:S(2)}, u32[]{:S(2)}) %collective-permute-start.33) | collective-permute-done | bytes 557088 | tf_op jit(solution)/shard_map/ppermute | solution.py:215
  434.4 6.1 %collective-permute-done.59 = bf16[4,34,1088]{2,1,0:T(8,128)(2,1)S(1)} collective-permute-done((bf16[4,34,1088]{2,1,0:T(8,128)(2,1)S(1)}, bf16[4,34,1088]{2,1,0:T(8,128)(2,1)S(1)}, u32[]{:S(2)}, u32[]{:S(2)}) %collective-permute-start.59) | collective-permute-done | bytes 295968 | tf_op jit(solution)/shard_map/ppermute | solution.py:279
  457.2 4.8 collective-permute-start.56
  477.4 6.2 %collective-permute-start.85 = (f32[34,960]{1,0:T(8,128)}, f32[34,960]{1,0:T(8,128)S(1)}, u32[]{:S(2)}, u32[]{:S(2)}) collective-permute-start(f32[34,960]{1,0:T(8,128)} %get-tuple-element.163), channel_id=1, source_target_pairs={{0,1},{1,2},{2,3},{3,0},{4,5},{5,6},{6,7},{7,4},{8,9},{9,10},{10,1... | collective-permute-start | bytes 391688 | tf_op jit(solution)/shard_map/ppermute | solution.py:215
  506.2 6.0 %collective-permute-start.78 = (f32[16,1088]{1,0:T(8,128)S(1)}, f32[16,1088]{1,0:T(8,128)S(1)}, u32[]{:S(2)}, u32[]{:S(2)}) collective-permute-start(f32[16,1088]{1,0:T(8,128)S(1)} %add_add_fusion.4), channel_id=1, source_target_pairs={{0,64},{4,68},{8,72},{12,76},{16,80},{20,84},{24,88},{28,92},{32,9... | collective-permute-start | bytes 208904 | tf_op jit(solution)/shard_map/ppermute | solution.py:296
  (456 shorter events, 295.9 us)
Async XLA Ops:
  7.2 66.1 %all-gather.6.cloned.1.call-start = ((), (), s32[]{:S(2)}) async-start(), calls=%async_computation | async-start | bytes 2703360 | tf_op jit(solution)/shard_map/all_gather | solution.py:362
  21.7 101.5 %all-gather.8.cloned.1.call-start = ((), (), s32[]{:S(2)}) async-start(), calls=%async_computation.1 | async-start | bytes 8785920 | tf_op jit(solution)/shard_map/all_gather | solution.py:367
  23.8 29.9 %collective-permute-start.3 = (bf16[256,1088]{0,1:T(8,128)(2,1)S(1)}, bf16[256,1088]{0,1:T(8,128)(2,1)}, u32[]{:S(2)}, u32[]{:S(2)}) collective-permute-start(bf16[256,1088]{0,1:T(8,128)(2,1)S(1)} %bitcast.341), channel_id=1, source_target_pairs={{0,3},{1,0},{2,1},{3,2},{4,7},{5,4},{6,5},{7,6},{8,11},{9,8},{10,9... | collective-permute-start | bytes 1671176 | tf_op jit(solution)/shard_map/ppermute | solution.py:215
  51.4 51.5 %collective-permute-start.21 = (bf16[256,1088]{0,1:T(8,128)(2,1)}, bf16[256,1088]{0,1:T(8,128)(2,1)}, u32[]{:S(2)}, u32[]{:S(2)}) collective-permute-start(bf16[256,1088]{0,1:T(8,128)(2,1)} %bitcast.38), channel_id=1, source_target_pairs={{0,3},{1,0},{2,1},{3,2},{4,7},{5,4},{6,5},{7,6},{8,11},{9,8},{10,9... | collective-permute-start | bytes 1671176 | tf_op jit(solution)/shard_map/ppermute | solution.py:215
  51.5 47.7 %collective-permute-start.22 = (bf16[256,1088]{0,1:T(8,128)(2,1)}, bf16[256,1088]{0,1:T(8,128)(2,1)}, u32[]{:S(2)}, u32[]{:S(2)}) collective-permute-start(bf16[256,1088]{0,1:T(8,128)(2,1)} %bitcast.38), channel_id=1, source_target_pairs={{0,1},{1,2},{2,3},{3,0},{4,5},{5,6},{6,7},{7,4},{8,9},{9,10},{10,1... | collective-permute-start | bytes 1671176 | tf_op jit(solution)/shard_map/ppermute | solution.py:215
  53.6 18.4 %collective-permute-start.5 = (bf16[128,1088]{0,1:T(8,128)(2,1)S(1)}, bf16[128,1088]{0,1:T(8,128)(2,1)S(1)}, u32[]{:S(2)}, u32[]{:S(2)}) collective-permute-start(bf16[128,1088]{0,1:T(8,128)(2,1)S(1)} %slice.314), channel_id=1, source_target_pairs={{0,1},{1,2},{2,3},{3,0},{4,5},{5,6},{6,7},{7,4},{8,9},{9,10},{10,1... | collective-permute-start | bytes 835592 | tf_op jit(solution)/shard_map/ppermute | solution.py:215
  54.7 17.4 %collective-permute-start.6 = (bf16[128,1088]{0,1:T(8,128)(2,1)S(1)}, bf16[128,1088]{0,1:T(8,128)(2,1)S(1)}, u32[]{:S(2)}, u32[]{:S(2)}) collective-permute-start(bf16[128,1088]{0,1:T(8,128)(2,1)S(1)} %slice.315), channel_id=1, source_target_pairs={{0,3},{1,0},{2,1},{3,2},{4,7},{5,4},{6,5},{7,6},{8,11},{9,8},{10,9... | collective-permute-start | bytes 835592 | tf_op jit(solution)/shard_map/ppermute | solution.py:215
  101.0 43.6 %collective-permute-start.23 = (bf16[128,1088]{0,1:T(8,128)(2,1)}, bf16[128,1088]{0,1:T(8,128)(2,1)}, u32[]{:S(2)}, u32[]{:S(2)}) collective-permute-start(bf16[128,1088]{0,1:T(8,128)(2,1)} %slice.335), channel_id=1, source_target_pairs={{0,1},{1,2},{2,3},{3,0},{4,5},{5,6},{6,7},{7,4},{8,9},{9,10},{10,1... | collective-permute-start | bytes 835592 | tf_op jit(solution)/shard_map/ppermute | solution.py:215
  104.6 41.7 %collective-permute-start.24 = (bf16[128,1088]{0,1:T(8,128)(2,1)}, bf16[128,1088]{0,1:T(8,128)(2,1)}, u32[]{:S(2)}, u32[]{:S(2)}) collective-permute-start(bf16[128,1088]{0,1:T(8,128)(2,1)} %slice.336), channel_id=1, source_target_pairs={{0,3},{1,0},{2,1},{3,2},{4,7},{5,4},{6,5},{7,6},{8,11},{9,8},{10,9... | collective-permute-start | bytes 835592 | tf_op jit(solution)/shard_map/ppermute | solution.py:215
  141.8 31.8 %collective-permute-start.14 = (bf16[256,1088]{0,1:T(8,128)(2,1)}, bf16[256,1088]{0,1:T(8,128)(2,1)}, u32[]{:S(2)}, u32[]{:S(2)}) collective-permute-start(bf16[256,1088]{0,1:T(8,128)(2,1)} %get-tuple-element.77), channel_id=1, source_target_pairs={{0,3},{1,0},{2,1},{3,2},{4,7},{5,4},{6,5},{7,6},{8,11},{9,8},{10,9... | collective-permute-start | bytes 1671176 | tf_op jit(solution)/shard_map/ppermute | solution.py:215
  155.3 24.4 %collective-permute-start.16 = (bf16[128,1088]{0,1:T(8,128)(2,1)}, bf16[128,1088]{0,1:T(8,128)(2,1)}, u32[]{:S(2)}, u32[]{:S(2)}) collective-permute-start(bf16[128,1088]{0,1:T(8,128)(2,1)} %slice.327), channel_id=1, source_target_pairs={{0,1},{1,2},{2,3},{3,0},{4,5},{5,6},{6,7},{7,4},{8,9},{9,10},{10,1... | collective-permute-start | bytes 835592 | tf_op jit(solution)/shard_map/ppermute | solution.py:215
  232.2 136.5 %collective-permute-start.65 = (bf16[4,4,136,272]{3,2,1,0:T(8,128)(2,1)}, bf16[4,4,136,272]{3,2,1,0:T(8,128)(2,1)}, u32[]{:S(2)}, u32[]{:S(2)}) collective-permute-start(bf16[4,4,136,272]{3,2,1,0:T(8,128)(2,1)} %bitcast.315), channel_id=1, source_target_pairs={{0,4},{4,0},{8,12},{12,8},{16,20},{20,16},{24,28},{28,24},{32,36},... | collective-permute-start | bytes 3551240 | tf_op jit(solution)/shard_map/ppermute | solution.py:266
  240.0 125.1 %collective-permute-start.58 = (bf16[4,4,34,1088]{3,1,2,0:T(4,128)(2,1)}, bf16[4,4,34,1088]{3,1,2,0:T(4,128)(2,1)}, u32[]{:S(2)}, u32[]{:S(2)}) collective-permute-start(bf16[4,4,34,1088]{3,1,2,0:T(4,128)(2,1)} %bitcast.316), channel_id=1, source_target_pairs={{0,4},{4,0},{8,12},{12,8},{16,20},{20,16},{24,28},{28,24},{32,36},... | collective-permute-start | bytes 3551240 | tf_op jit(solution)/shard_map/ppermute | solution.py:266
  242.2 28.3 %collective-permute-start.26 = (bf16[256,1088]{0,1:T(8,128)(2,1)S(1)}, bf16[256,1088]{0,1:T(8,128)(2,1)S(1)}, u32[]{:S(2)}, u32[]{:S(2)}) collective-permute-start(bf16[256,1088]{0,1:T(8,128)(2,1)S(1)} %get-tuple-element.95), channel_id=1, source_target_pairs={{0,2},{1,3},{2,0},{3,1},{4,6},{5,7},{6,4},{7,5},{8,10},{9,11},{10,... | collective-permute-start | bytes 1671176 | tf_op jit(solution)/shard_map/ppermute | solution.py:215
  245.1 26.1 %collective-permute-start.27 = (bf16[256,1088]{0,1:T(8,128)(2,1)S(1)}, bf16[256,1088]{0,1:T(8,128)(2,1)S(1)}, u32[]{:S(2)}, u32[]{:S(2)}) collective-permute-start(bf16[256,1088]{0,1:T(8,128)(2,1)S(1)} %get-tuple-element.94), channel_id=1, source_target_pairs={{0,3},{1,0},{2,1},{3,2},{4,7},{5,4},{6,5},{7,6},{8,11},{9,8},{10,9... | collective-permute-start | bytes 1671176 | tf_op jit(solution)/shard_map/ppermute | solution.py:215
  256.5 25.9 %collective-permute-start.18 = (bf16[256,1088]{0,1:T(8,128)(2,1)S(1)}, bf16[256,1088]{0,1:T(8,128)(2,1)S(1)}, u32[]{:S(2)}, u32[]{:S(2)}) collective-permute-start(bf16[256,1088]{0,1:T(8,128)(2,1)S(1)} %get-tuple-element.96), channel_id=1, source_target_pairs={{0,1},{1,2},{2,3},{3,0},{4,5},{5,6},{6,7},{7,4},{8,9},{9,10},{10,1... | collective-permute-start | bytes 1671176 | tf_op jit(solution)/shard_map/ppermute | solution.py:215
  270.6 22.9 %collective-permute-start.19 = (bf16[256,1088]{0,1:T(8,128)(2,1)S(1)}, bf16[256,1088]{0,1:T(8,128)(2,1)S(1)}, u32[]{:S(2)}, u32[]{:S(2)}) collective-permute-start(bf16[256,1088]{0,1:T(8,128)(2,1)S(1)} %get-tuple-element.98), channel_id=1, source_target_pairs={{0,2},{1,3},{2,0},{3,1},{4,6},{5,7},{6,4},{7,5},{8,10},{9,11},{10,... | collective-permute-start | bytes 1671176 | tf_op jit(solution)/shard_map/ppermute | solution.py:215
  271.2 22.3 %collective-permute-start.20 = (bf16[256,1088]{0,1:T(8,128)(2,1)S(1)}, bf16[256,1088]{0,1:T(8,128)(2,1)S(1)}, u32[]{:S(2)}, u32[]{:S(2)}) collective-permute-start(bf16[256,1088]{0,1:T(8,128)(2,1)S(1)} %get-tuple-element.97), channel_id=1, source_target_pairs={{0,3},{1,0},{2,1},{3,2},{4,7},{5,4},{6,5},{7,6},{8,11},{9,8},{10,9... | collective-permute-start | bytes 1671176 | tf_op jit(solution)/shard_map/ppermute | solution.py:215
  311.7 42.4 %collective-permute-start.48 = (bf16[1088,272]{0,1:T(8,128)(2,1)}, bf16[1088,272]{0,1:T(8,128)(2,1)}, u32[]{:S(2)}, u32[]{:S(2)}) collective-permute-start(bf16[1088,272]{0,1:T(8,128)(2,1)} %get-tuple-element.87), channel_id=1, source_target_pairs={{0,3},{1,0},{2,1},{3,2},{4,7},{5,4},{6,5},{7,6},{8,11},{9,8},{10,9... | collective-permute-start | bytes 1775624 | tf_op jit(solution)/shard_map/ppermute | solution.py:215
  315.5 38.6 %collective-permute-start.49 = (bf16[1088,272]{0,1:T(8,128)(2,1)}, bf16[1088,272]{0,1:T(8,128)(2,1)}, u32[]{:S(2)}, u32[]{:S(2)}) collective-permute-start(bf16[1088,272]{0,1:T(8,128)(2,1)} %get-tuple-element.89), channel_id=1, source_target_pairs={{0,2},{1,3},{2,0},{3,1},{4,6},{5,7},{6,4},{7,5},{8,10},{9,11},{10,... | collective-permute-start | bytes 1775624 | tf_op jit(solution)/shard_map/ppermute | solution.py:215
  316.2 38.4 %collective-permute-start.50 = (bf16[1088,272]{0,1:T(8,128)(2,1)}, bf16[1088,272]{0,1:T(8,128)(2,1)}, u32[]{:S(2)}, u32[]{:S(2)}) collective-permute-start(bf16[1088,272]{0,1:T(8,128)(2,1)} %get-tuple-element.88), channel_id=1, source_target_pairs={{0,1},{1,2},{2,3},{3,0},{4,5},{5,6},{6,7},{7,4},{8,9},{9,10},{10,1... | collective-permute-start | bytes 1775624 | tf_op jit(solution)/shard_map/ppermute | solution.py:215
  354.1 46.9 %collective-permute-start.34 = (bf16[4,4,34,512]{3,1,2,0:T(4,128)(2,1)}, bf16[4,4,34,512]{3,1,2,0:T(4,128)(2,1)}, u32[]{:S(2)}, u32[]{:S(2)}) collective-permute-start(bf16[4,4,34,512]{3,1,2,0:T(4,128)(2,1)} %bitcast.318), channel_id=1, source_target_pairs={{0,4},{4,0},{8,12},{12,8},{16,20},{20,16},{24,28},{28,24},{32,36},... | collective-permute-start | bytes 1671176 | tf_op jit(solution)/shard_map/ppermute | solution.py:266
  354.1 17.9 %collective-permute-start.41 = (bf16[4,4,34,448]{3,1,2,0:T(4,128)(2,1)}, bf16[4,4,34,448]{3,1,2,0:T(4,128)(2,1)}, u32[]{:S(2)}, u32[]{:S(2)}) collective-permute-start(bf16[4,4,34,448]{3,1,2,0:T(4,128)(2,1)} %bitcast.317), channel_id=1, source_target_pairs={{0,4},{4,0},{8,12},{12,8},{16,20},{20,16},{24,28},{28,24},{32,36},... | collective-permute-start | bytes 1462280 | tf_op jit(solution)/shard_map/ppermute | solution.py:266
  354.6 20.1 %collective-permute-start.31 = (bf16[256,1088]{0,1:T(8,128)(2,1)}, bf16[256,1088]{0,1:T(8,128)(2,1)}, u32[]{:S(2)}, u32[]{:S(2)}) collective-permute-start(bf16[256,1088]{0,1:T(8,128)(2,1)} %get-tuple-element.90), channel_id=1, source_target_pairs={{0,1},{1,2},{2,3},{3,0},{4,5},{5,6},{6,7},{7,4},{8,9},{9,10},{10,1... | collective-permute-start | bytes 1671176 | tf_op jit(solution)/shard_map/ppermute | solution.py:215
  365.2 18.0 %collective-permute-start.32 = (bf16[256,1088]{0,1:T(8,128)(2,1)}, bf16[256,1088]{0,1:T(8,128)(2,1)S(1)}, u32[]{:S(2)}, u32[]{:S(2)}) collective-permute-start(bf16[256,1088]{0,1:T(8,128)(2,1)} %get-tuple-element.92), channel_id=1, source_target_pairs={{0,2},{1,3},{2,0},{3,1},{4,6},{5,7},{6,4},{7,5},{8,10},{9,11},{10,... | collective-permute-start | bytes 1671176 | tf_op jit(solution)/shard_map/ppermute | solution.py:215
  368.8 23.1 %collective-permute-start.33 = (bf16[256,1088]{0,1:T(8,128)(2,1)S(1)}, bf16[256,1088]{0,1:T(8,128)(2,1)S(1)}, u32[]{:S(2)}, u32[]{:S(2)}) collective-permute-start(bf16[256,1088]{0,1:T(8,128)(2,1)S(1)} %copy-done.29), channel_id=1, source_target_pairs={{0,3},{1,0},{2,1},{3,2},{4,7},{5,4},{6,5},{7,6},{8,11},{9,8},{10,9... | collective-permute-start | bytes 1671176 | tf_op jit(solution)/shard_map/ppermute | solution.py:215
  372.1 53.4 %collective-permute-start.51 = (bf16[4,4,34,272]{3,2,1,0:T(8,128)(2,1)S(1)}, bf16[4,4,34,272]{3,2,1,0:T(8,128)(2,1)S(1)}, u32[]{:S(2)}, u32[]{:S(2)}) collective-permute-start(bf16[4,4,34,272]{3,2,1,0:T(8,128)(2,1)S(1)} %dynamic-slice_bitcast_fusion), channel_id=1, source_target_pairs={{0,4},{4,0},{8,12},{12,8},{16,20},{20,16},{24,28},{28,24},{32,36},... | collective-permute-start | bytes 887816 | tf_op jit(solution)/shard_map/ppermute | solution.py:266
  374.7 72.9 %collective-permute-start.66 = (bf16[4,136,272]{2,1,0:T(8,128)(2,1)S(1)}, bf16[4,136,272]{2,1,0:T(8,128)(2,1)S(1)}, u32[]{:S(2)}, u32[]{:S(2)}) collective-permute-start(bf16[4,136,272]{2,1,0:T(8,128)(2,1)S(1)} %get-tuple-element.103), channel_id=1, source_target_pairs={{0,32},{4,36},{8,40},{12,44},{16,48},{20,52},{24,56},{28,60},{32,6... | collective-permute-start | bytes 887816 | tf_op jit(solution)/shard_map/ppermute | solution.py:279
  383.2 21.7 %collective-permute-start.42 = (bf16[4,34,448]{2,0,1:T(4,128)(2,1)S(1)}, bf16[4,34,448]{2,0,1:T(4,128)(2,1)S(1)}, u32[]{:S(2)}, u32[]{:S(2)}) collective-permute-start(bf16[4,34,448]{2,0,1:T(4,128)(2,1)S(1)} %bitcast.353), channel_id=1, source_target_pairs={{0,32},{4,36},{8,40},{12,44},{16,48},{20,52},{24,56},{28,60},{32,6... | collective-permute-start | bytes 365576 | tf_op jit(solution)/shard_map/ppermute | solution.py:279
  419.7 30.5 %collective-permute-start.67 = (bf16[4,136,272]{2,1,0:T(8,128)(2,1)S(1)}, bf16[4,136,272]{2,1,0:T(8,128)(2,1)S(1)}, u32[]{:S(2)}, u32[]{:S(2)}) collective-permute-start(bf16[4,136,272]{2,1,0:T(8,128)(2,1)S(1)} %get-tuple-element.105), channel_id=1, source_target_pairs={{0,64},{4,68},{8,72},{12,76},{16,80},{20,84},{24,88},{28,92},{32,9... | collective-permute-start | bytes 887816 | tf_op jit(solution)/shard_map/ppermute | solution.py:279
  450.2 36.3 %collective-permute-start.83 = (f32[34,960]{1,0:T(8,128)}, f32[34,960]{1,0:T(8,128)S(1)}, u32[]{:S(2)}, u32[]{:S(2)}) collective-permute-start(f32[34,960]{1,0:T(8,128)} %get-tuple-element.163), channel_id=1, source_target_pairs={{0,3},{1,0},{2,1},{3,2},{4,7},{5,4},{6,5},{7,6},{8,11},{9,8},{10,9... | collective-permute-start | bytes 391688 | tf_op jit(solution)/shard_map/ppermute | solution.py:215
  454.0 32.6 %collective-permute-start.84 = (f32[34,960]{1,0:T(8,128)}, f32[34,960]{1,0:T(8,128)S(1)}, u32[]{:S(2)}, u32[]{:S(2)}) collective-permute-start(f32[34,960]{1,0:T(8,128)} %get-tuple-element.163), channel_id=1, source_target_pairs={{0,2},{1,3},{2,0},{3,1},{4,6},{5,7},{6,4},{7,5},{8,10},{9,11},{10,... | collective-permute-start | bytes 391688 | tf_op jit(solution)/shard_map/ppermute | solution.py:215
  (103 other events, 954.5 us)
Sparse Core Ops, SparseCore 0:
  21.9 44.7 all-gather.5
  69.6 52.5 all-gather.7
